TPU v7x, 32 devices: a whole 2x2x4 slice. The times are simulated.
32 devices in a mesh: expert: 2 (over x), shard: 4 (over z), dp: 4 (over y, core).
Axes of the slice: x: 2, y: 2, z: 4, core: 2. Of those that a mesh axis runs over, the one named last changes fastest.
Arguments:
- tokens: bfloat16 [4096, 768], P(('expert', 'shard', 'dp')), may hold values from -6 to 6
- lengths: int32 [32, 4], P(('expert', 'shard', 'dp')), may hold values from 1 to 64, 128 in all within a row
- routes: int32 [4096, 1], P(('expert', 'shard', 'dp')), may hold values from 0 to 1
- buckets: int32 [255], replicated, may hold values from 0 to 31
- bias_table: float32 [32, 12], replicated, may hold values from -5 to 5
- projection: bfloat16 [2, 768, 2304], P(None, ('shard', 'dp')), may hold values from -0.21875 to 0.21875
- collector: bfloat16 [2, 768, 768], P(None, ('shard', 'dp')), may hold values from -0.875 to 0.875
- router: bfloat16 [2, 768, 2], P(None, ('shard', 'dp')), may hold values from -0.15625 to 0.15625
- scales: bfloat16 [2, 768, 2], P(None, ('shard', 'dp')), may hold values from 0.099609375 to 1.8984375
- upward: bfloat16 [2, 2, 768, 3072], P(None, 'expert', None, 'shard'), may hold values from -0.21875 to 0.21875
- downward: bfloat16 [2, 2, 3072, 768], P(None, 'expert', 'shard'), may hold values from -0.875 to 0.875
- cotangent: bfloat16 [4096, 768], P(('expert', 'shard', 'dp')), may hold values from -6 to 6
Outputs:
- activations: bfloat16 [4096, 768], P(('expert', 'shard', 'dp'))
- tokens_grad: float32 [4096, 768], P(('expert', 'shard', 'dp'))
- projection_grad: float32 [2, 768, 2304], P(None, ('shard', 'dp'))
- collector_grad: float32 [2, 768, 768], P(None, ('shard', 'dp'))
- router_grad: float32 [2, 768, 2], P(None, ('shard', 'dp'))
- scales_grad: float32 [2, 768, 2], P(None, ('shard', 'dp'))
- upward_grad: float32 [2, 2, 768, 3072], P(None, 'expert', 'dp', 'shard')
- downward_grad: float32 [2, 2, 3072, 768], P(None, 'expert', 'shard', 'dp')
- table_grad: float32 [32, 12], replicated
Inputs may be any that keep to these rules, and one draw needn't show every extreme that they name: `lengths`: each row sums to 128; the longest in every row is 64. `routes`: every expert is named by some token.
All inputs are finite; a program needn't handle non-finite values.
Results may differ from a plain program's by a relative error of at most 0.029.
Values may be sent and summed in bfloat16 or wider, within the bound.
A program may use at most 128 MiB of HBM per device.

v0:
```python
import jax
import jax.numpy as jnp
from jax import lax
from jax.sharding import PartitionSpec as P

HEADS = 12
HEAD_DIM = 64


EPSILON = 1e-06
NEG_FILL = -1e30
HIGHEST = lax.Precision.HIGHEST


def rms_forward(inputs, gain_vector):
    scale_rows = lax.rsqrt(jnp.mean(inputs * inputs, axis=-1, keepdims=True) + EPSILON)
    normed = inputs * scale_rows
    return (normed * gain_vector, normed, scale_rows)


def rms_backward(grad_output, gain_vector, normed, scale_rows):
    grad_normed = grad_output * gain_vector
    grad_gain = jnp.sum(grad_output * normed, axis=0)
    grad_inputs = scale_rows * (
        grad_normed - normed * jnp.mean(grad_normed * normed, axis=-1, keepdims=True)
    )
    return (grad_inputs, grad_gain)


def send_rows(buffer):
    return lax.all_to_all(buffer, "expert", split_axis=0, concat_axis=0, tiled=True)


def return_rows(buffer):
    return lax.all_to_all(buffer, "expert", split_axis=0, concat_axis=0, tiled=True)


def spread_rows(arrived):
    return lax.all_gather(arrived, "shard", axis=0, tiled=True)


def sum_hidden(partial_value):
    return lax.psum_scatter(
        partial_value.astype(jnp.bfloat16), "shard", scatter_dimension=0, tiled=True
    ).astype(jnp.float32)


def fetch_mixer(projection, collector, router, scales, layer):
    return (
        lax.all_gather(projection[layer], ("shard", "dp"), axis=0, tiled=True),
        lax.all_gather(collector[layer], ("shard", "dp"), axis=0, tiled=True),
        lax.all_gather(router[layer], ("shard", "dp"), axis=0, tiled=True),
        lax.all_gather(scales[layer], ("shard", "dp"), axis=0, tiled=True),
    )


def fetch_again(projection, collector, router, scales, layer):
    return (
        lax.all_gather(projection[layer], ("shard", "dp"), axis=0, tiled=True),
        lax.all_gather(collector[layer], ("shard", "dp"), axis=0, tiled=True),
        lax.all_gather(router[layer], ("shard", "dp"), axis=0, tiled=True),
        lax.all_gather(scales[layer], ("shard", "dp"), axis=0, tiled=True),
    )


def score_heads(queries, key_heads, bias_heads, same_segment):
    scores = (
        jnp.einsum("thd,shd->hts", queries, key_heads, preferred_element_type=jnp.float32)
        * HEAD_DIM ** (-0.5)
        + bias_heads
    )
    return jnp.where(same_segment[None], scores, NEG_FILL)


def offsets_to_pairs(offset_rows, tokens_dev):
    heads_all = offset_rows.shape[0]
    padded = jnp.pad(offset_rows, ((0, 0), (0, 1)))
    tiled = jnp.tile(padded, (1, tokens_dev))
    window = tiled[:, tokens_dev - 1 : tokens_dev - 1 + tokens_dev * (2 * tokens_dev - 1)]
    return window.reshape(heads_all, tokens_dev, 2 * tokens_dev - 1)[:, :, :tokens_dev]


def pairs_to_offsets(pair_values, tokens_dev):
    heads_all = pair_values.shape[0]
    widened = jnp.pad(pair_values, ((0, 0), (0, 0), (0, tokens_dev - 1)))
    flat = widened.reshape(heads_all, tokens_dev * (2 * tokens_dev - 1))
    flat = jnp.pad(flat, ((0, 0), (tokens_dev - 1, 1)))
    folded = jnp.sum(flat.reshape(heads_all, tokens_dev, 2 * tokens_dev), axis=1)
    return folded[:, : 2 * tokens_dev - 1]


def body(
    tokens,
    lengths,
    routes,
    buckets,
    bias_table,
    projection,
    collector,
    router,
    scales,
    upward,
    downward,
    cotangent,
):
    tokens_dev, model_width = tokens.shape
    layers = projection.shape[0]
    experts = router.shape[2]
    capacity = 5 * tokens_dev // (4 * experts)
    buckets_all = bias_table.shape[0]
    head_scale = HEAD_DIM ** (-0.5)
    places = jnp.arange(tokens_dev, dtype=jnp.int32)
    bounds = jnp.cumsum(lengths[0])
    segment = jnp.sum((places[:, None] >= bounds[None, :]).astype(jnp.int32), axis=1)
    same_segment = segment[:, None] == segment[None, :]
    offset_hot = (buckets[:, None] == jnp.arange(buckets_all, dtype=jnp.int32)[None, :]).astype(
        jnp.float32
    )
    offset_bias = jnp.dot(offset_hot, bias_table, precision=HIGHEST).T
    bias_heads = offsets_to_pairs(offset_bias, tokens_dev)
    chosen = routes[:, 0]
    route_hot = (chosen[:, None] == jnp.arange(experts, dtype=jnp.int32)[None, :]).astype(jnp.int32)
    position = jnp.sum(jnp.cumsum(route_hot, axis=0) * route_hot, axis=1) - 1
    retained = (position < capacity).astype(jnp.float32)
    slot_index = chosen * capacity + position
    slot_hot = (
        slot_index[:, None] == jnp.arange(experts * capacity, dtype=jnp.int32)[None, :]
    ).astype(jnp.float32)
    slot_hot = (slot_hot * retained[:, None]).astype(jnp.bfloat16)
    slot_back = slot_hot.T
    route_float = route_hot.astype(jnp.float32)
    residual = tokens.astype(jnp.float32)
    stored = []
    for layer in range(layers):
        fetched = fetch_mixer(projection, collector, router, scales, layer)
        proj_full, collect_full, router_full, scales_full = fetched
        gain_one = scales_full[:, 0].astype(jnp.float32)
        gain_two = scales_full[:, 1].astype(jnp.float32)
        normed_one, base_one, scale_one = rms_forward(residual, gain_one)
        hidden_one = normed_one.astype(jnp.bfloat16)
        packed = jnp.dot(hidden_one, proj_full, preferred_element_type=jnp.float32).astype(
            jnp.bfloat16
        )
        queries = packed[:, :model_width].reshape(tokens_dev, HEADS, HEAD_DIM)
        key_heads = packed[:, model_width : 2 * model_width].reshape(tokens_dev, HEADS, HEAD_DIM)
        value_heads = packed[:, 2 * model_width :].reshape(tokens_dev, HEADS, HEAD_DIM)
        scores = score_heads(queries, key_heads, bias_heads, same_segment)
        row_peak = jnp.max(scores, axis=-1, keepdims=True)
        log_total = row_peak + jnp.log(jnp.sum(jnp.exp(scores - row_peak), axis=-1, keepdims=True))
        attention = jnp.exp(scores - log_total)
        mixed_heads = jnp.einsum(
            "hts,shd->thd",
            attention.astype(jnp.bfloat16),
            value_heads,
            preferred_element_type=jnp.float32,
        )
        mixed_heads = mixed_heads.reshape(tokens_dev, model_width).astype(jnp.bfloat16)
        middle = residual + jnp.dot(mixed_heads, collect_full, preferred_element_type=jnp.float32)
        normed_two, base_two, scale_two = rms_forward(middle, gain_two)
        router_float = router_full.astype(jnp.float32)
        logits = jnp.dot(normed_two, router_float, precision=HIGHEST)
        gate_probs = jax.nn.softmax(logits, axis=-1)
        gate_value = jnp.sum(gate_probs * route_float, axis=1) * retained
        sent = normed_two.astype(jnp.bfloat16)
        buffer = jnp.dot(slot_back, sent, preferred_element_type=jnp.float32).astype(jnp.bfloat16)
        arrived = send_rows(buffer.reshape(experts, capacity, model_width)).reshape(
            experts * capacity, model_width
        )
        rows_all = spread_rows(arrived)
        hidden_pre = jnp.dot(rows_all, upward[layer, 0], preferred_element_type=jnp.float32)
        hidden_act = jax.nn.gelu(hidden_pre).astype(jnp.bfloat16)
        partial_value = jnp.dot(hidden_act, downward[layer, 0], preferred_element_type=jnp.float32)
        expert_sum = (
            sum_hidden(partial_value).astype(jnp.bfloat16).reshape(experts, capacity, model_width)
        )
        returned = return_rows(expert_sum).reshape(experts * capacity, model_width)
        expert_tokens = jnp.dot(slot_hot, returned, preferred_element_type=jnp.float32)
        residual = middle + gate_value[:, None] * expert_tokens
        stored.append(
            dict(
                fetched=fetched,
                base_one=base_one,
                scale_one=scale_one,
                hidden_one=hidden_one,
                queries=queries,
                key_heads=key_heads,
                value_heads=value_heads,
                log_total=log_total,
                mixed_heads=mixed_heads,
                base_two=base_two,
                scale_two=scale_two,
                normed_two=normed_two,
                gate_probs=gate_probs,
                gate_value=gate_value,
                rows_all=rows_all,
                hidden_pre=hidden_pre,
                hidden_act=hidden_act,
                expert_tokens=expert_tokens,
            )
        )
    grad_residual = cotangent.astype(jnp.float32)
    offset_total = jnp.zeros((HEADS, 2 * tokens_dev - 1), jnp.float32)
    proj_grads, collect_grads, router_grads, scale_grads, up_grads, down_grads = (
        [],
        [],
        [],
        [],
        [],
        [],
    )
    for layer in reversed(range(layers)):
        saved_layer = stored[layer]
        proj_full, collect_full, router_full, scales_full = fetch_again(
            projection, collector, router, scales, layer
        )
        gain_one = scales_full[:, 0].astype(jnp.float32)
        gain_two = scales_full[:, 1].astype(jnp.float32)
        router_float = router_full.astype(jnp.float32)
        gate_value = saved_layer["gate_value"]
        gate_probs = saved_layer["gate_probs"]
        grad_gate = jnp.sum(grad_residual * saved_layer["expert_tokens"], axis=1)
        grad_tokens_out = (gate_value[:, None] * grad_residual).astype(jnp.bfloat16)
        grad_buffer = jnp.dot(
            slot_back, grad_tokens_out, preferred_element_type=jnp.float32
        ).astype(jnp.bfloat16)
        grad_arrived = send_rows(grad_buffer.reshape(experts, capacity, model_width)).reshape(
            experts * capacity, model_width
        )
        grad_spread = spread_rows(grad_arrived)
        grad_act = jnp.dot(grad_spread, downward[layer, 0].T, preferred_element_type=jnp.float32)
        gelu_value, gelu_pull = jax.vjp(jax.nn.gelu, saved_layer["hidden_pre"])
        grad_pre = gelu_pull(grad_act)[0].astype(jnp.bfloat16)
        grad_down_t = jnp.dot(
            grad_spread.T, saved_layer["hidden_act"], preferred_element_type=jnp.float32
        )
        grad_up = jnp.dot(saved_layer["rows_all"].T, grad_pre, preferred_element_type=jnp.float32)
        grad_sent_part = jnp.dot(grad_pre, upward[layer, 0].T, preferred_element_type=jnp.float32)
        grad_sent = (
            sum_hidden(grad_sent_part).astype(jnp.bfloat16).reshape(experts, capacity, model_width)
        )
        grad_back = return_rows(grad_sent).reshape(experts * capacity, model_width)
        grad_normed_two = jnp.dot(slot_hot, grad_back, preferred_element_type=jnp.float32)
        grad_gprobs = (grad_gate * retained)[:, None] * route_float
        grad_logits = gate_probs * (
            grad_gprobs - jnp.sum(grad_gprobs * gate_probs, axis=1, keepdims=True)
        )
        grad_router = jnp.dot(saved_layer["normed_two"].T, grad_logits, precision=HIGHEST)
        grad_normed_two = grad_normed_two + jnp.dot(grad_logits, router_float.T, precision=HIGHEST)
        grad_mid_norm, grad_gain_two = rms_backward(
            grad_normed_two, gain_two, saved_layer["base_two"], saved_layer["scale_two"]
        )
        grad_middle = grad_residual + grad_mid_norm
        grad_branch = grad_middle.astype(jnp.bfloat16)
        grad_collect = jnp.dot(
            saved_layer["mixed_heads"].T, grad_branch, preferred_element_type=jnp.float32
        )
        grad_mixed = jnp.dot(
            grad_branch, collect_full.T, preferred_element_type=jnp.float32
        ).astype(jnp.bfloat16)
        grad_mixed = grad_mixed.reshape(tokens_dev, HEADS, HEAD_DIM)
        queries = saved_layer["queries"]
        key_heads = saved_layer["key_heads"]
        value_heads = saved_layer["value_heads"]
        scores = score_heads(queries, key_heads, bias_heads, same_segment)
        attention = jnp.exp(scores - saved_layer["log_total"])
        grad_values = jnp.einsum(
            "hts,thd->shd",
            attention.astype(jnp.bfloat16),
            grad_mixed,
            preferred_element_type=jnp.float32,
        )
        grad_attention = jnp.einsum(
            "thd,shd->hts", grad_mixed, value_heads, preferred_element_type=jnp.float32
        )
        grad_scores = attention * (
            grad_attention - jnp.sum(grad_attention * attention, axis=-1, keepdims=True)
        )
        grad_scores_low = grad_scores.astype(jnp.bfloat16)
        grad_queries = (
            jnp.einsum(
                "hts,shd->thd", grad_scores_low, key_heads, preferred_element_type=jnp.float32
            )
            * head_scale
        )
        grad_keys = (
            jnp.einsum("hts,thd->shd", grad_scores_low, queries, preferred_element_type=jnp.float32)
            * head_scale
        )
        offset_total = offset_total + pairs_to_offsets(
            grad_scores_low.astype(jnp.float32), tokens_dev
        )
        grad_packed = jnp.concatenate(
            [
                grad_queries.reshape(tokens_dev, model_width),
                grad_keys.reshape(tokens_dev, model_width),
                grad_values.reshape(tokens_dev, model_width),
            ],
            axis=1,
        ).astype(jnp.bfloat16)
        grad_proj = jnp.dot(
            saved_layer["hidden_one"].T, grad_packed, preferred_element_type=jnp.float32
        )
        grad_hidden_one = jnp.dot(grad_packed, proj_full.T, preferred_element_type=jnp.float32)
        grad_in_norm, grad_gain_one = rms_backward(
            grad_hidden_one, gain_one, saved_layer["base_one"], saved_layer["scale_one"]
        )
        grad_residual = grad_middle + grad_in_norm
        grad_scales = jnp.stack([grad_gain_one, grad_gain_two], axis=1)
        shares = (
            lax.psum_scatter(
                grad_proj.astype(jnp.bfloat16), ("shard", "dp"), scatter_dimension=0, tiled=True
            ).astype(jnp.float32),
            lax.psum_scatter(
                grad_collect.astype(jnp.bfloat16), ("shard", "dp"), scatter_dimension=0, tiled=True
            ).astype(jnp.float32),
            lax.psum_scatter(
                grad_router.astype(jnp.bfloat16), ("shard", "dp"), scatter_dimension=0, tiled=True
            ).astype(jnp.float32),
            lax.psum_scatter(
                grad_scales.astype(jnp.bfloat16), ("shard", "dp"), scatter_dimension=0, tiled=True
            ).astype(jnp.float32),
        )
        shares = (
            lax.psum(shares[0].astype(jnp.bfloat16), "expert").astype(jnp.float32),
            lax.psum(shares[1].astype(jnp.bfloat16), "expert").astype(jnp.float32),
            lax.psum(shares[2].astype(jnp.bfloat16), "expert").astype(jnp.float32),
            lax.psum(shares[3].astype(jnp.bfloat16), "expert").astype(jnp.float32),
        )
        expert_shares = (
            lax.psum_scatter(
                grad_up.astype(jnp.bfloat16), "dp", scatter_dimension=0, tiled=True
            ).astype(jnp.float32),
            lax.psum_scatter(
                grad_down_t.astype(jnp.bfloat16), "dp", scatter_dimension=0, tiled=True
            ).astype(jnp.float32),
        )
        proj_grads.insert(0, shares[0])
        collect_grads.insert(0, shares[1])
        router_grads.insert(0, shares[2])
        scale_grads.insert(0, shares[3])
        up_grads.insert(0, expert_shares[0][None])
        down_grads.insert(0, expert_shares[1].T[None])
    table_total = jnp.dot(offset_total, offset_hot, precision=HIGHEST).T
    table_sum = lax.psum(table_total, ("expert", "shard", "dp"))
    return (
        residual.astype(jnp.bfloat16),
        grad_residual,
        jnp.stack(proj_grads),
        jnp.stack(collect_grads),
        jnp.stack(router_grads),
        jnp.stack(scale_grads),
        jnp.stack(up_grads),
        jnp.stack(down_grads),
        table_sum,
    )


def solution(mesh):
    in_specs = (
        P(("expert", "shard", "dp"), None),
        P(("expert", "shard", "dp"), None),
        P(("expert", "shard", "dp"), None),
        P(),
        P(),
        P(None, ("shard", "dp"), None),
        P(None, ("shard", "dp"), None),
        P(None, ("shard", "dp"), None),
        P(None, ("shard", "dp"), None),
        P(None, "expert", None, "shard"),
        P(None, "expert", "shard", None),
        P(("expert", "shard", "dp"), None),
    )
    out_specs = (
        P(("expert", "shard", "dp"), None),
        P(("expert", "shard", "dp"), None),
        P(None, ("shard", "dp"), None),
        P(None, ("shard", "dp"), None),
        P(None, ("shard", "dp"), None),
        P(None, ("shard", "dp"), None),
        P(None, "expert", "dp", "shard"),
        P(None, "expert", "shard", "dp"),
        P(),
    )
    return jax.shard_map(body, mesh=mesh, in_specs=in_specs, out_specs=out_specs, check_vma=False)
```

profile of v0, /device:TPU:0, one launch (start us, length us, event | category | flops | bytes accessed | tf_op | source)
XLA Modules:
  0.0 1107.4 jit_solution(15067786199449726067)
XLA Ops:
  14.6 25.0 %all-gather = bf16[1,768,2]{2,0,1:T(2,128)(2,1)S(1)} all-gather(bf16[1,48,2]{2,0,1:T(2,128)(2,1)S(1)} %copy.167), channel_id=2, replica_groups=mesh['expert'=2,'shard'=4,'dp'=4] {'shard','dp'}, dimensions={1}, use_global_device_ids=true | all-gather | bytes 3264 | tf_op jit(solution)/shard_map/all_gather | solution.py:53
  65.4 36.2 %all-gather.15.cloned.1.call-done = bf16[1,768,768]{2,1,0:T(8,128)(2,1)} async-done(((bf16[1,48,768]{2,1,0:T(8,128)(2,1)}), bf16[1,768,768]{2,1,0:T(8,128)(2,1)}) %all-gather.15.cloned.1.call-update) | async-done | bytes 1179664 | tf_op jit(solution)/shard_map/all_gather | solution.py:51
  112.0 20.7 %all_gather.48 = bf16[640,768]{1,0:T(8,128)(2,1)S(1)} all-gather(bf16[160,768]{1,0:T(8,128)(2,1)S(1)} %bitcast.231), channel_id=1, replica_groups=mesh['expert'=2,'shard'=4,'dp'=4] {'shard'}, dimensions={0}, use_global_device_ids=true | all-gather | bytes 1228800 | tf_op jit(solution)/shard_map/all_gather | solution.py:39
  140.2 22.3 %all-gather.3 = bf16[1,768,2]{2,0,1:T(2,128)(2,1)S(1)} all-gather(bf16[1,48,2]{2,0,1:T(2,128)(2,1)S(1)} %copy.169), channel_id=5, replica_groups=mesh['expert'=2,'shard'=4,'dp'=4] {'shard','dp'}, dimensions={1}, use_global_device_ids=true | all-gather | bytes 3264 | tf_op jit(solution)/shard_map/all_gather | solution.py:52
  219.5 33.0 %all-gather.19.cloned.1.call-done = bf16[1,768,768]{2,1,0:T(8,128)(2,1)} async-done(((bf16[1,48,768]{2,1,0:T(8,128)(2,1)}), bf16[1,768,768]{2,1,0:T(8,128)(2,1)}) %all-gather.19.cloned.1.call-update) | async-done | bytes 1179664 | tf_op jit(solution)/shard_map/all_gather | solution.py:51
  262.9 20.7 %all_gather.53 = bf16[640,768]{1,0:T(8,128)(2,1)S(1)} all-gather(bf16[160,768]{1,0:T(8,128)(2,1)S(1)} %bitcast.232), channel_id=1, replica_groups=mesh['expert'=2,'shard'=4,'dp'=4] {'shard'}, dimensions={0}, use_global_device_ids=true | all-gather | bytes 1228800 | tf_op jit(solution)/shard_map/all_gather | solution.py:39
  289.2 22.1 %all-gather.7 = bf16[1,768,2]{2,0,1:T(2,128)(2,1)S(1)} all-gather(bf16[1,48,2]{2,0,1:T(2,128)(2,1)S(1)} %copy.171), channel_id=9, replica_groups=mesh['expert'=2,'shard'=4,'dp'=4] {'shard','dp'}, dimensions={1}, use_global_device_ids=true | all-gather | bytes 3264 | tf_op jit(solution)/shard_map/all_gather | solution.py:52
  334.3 19.7 %all_gather.54 = bf16[640,768]{1,0:T(8,128)(2,1)S(1)} all-gather(bf16[160,768]{1,0:T(8,128)(2,1)S(1)} %bitcast.233), channel_id=1, replica_groups=mesh['expert'=2,'shard'=4,'dp'=4] {'shard'}, dimensions={0}, use_global_device_ids=true | all-gather | bytes 1228800 | tf_op jit(solution)/shard_map/all_gather | solution.py:39
  360.8 25.0 %reduce-scatter.29.cloned.1.call-done = bf16[160,768]{1,0:T(8,128)(2,1)} async-done(((bf16[640,768]{1,0:T(8,128)(2,1)}), bf16[160,768]{1,0:T(8,128)(2,1)}) %reduce-scatter.29.cloned.1.call-update) | async-done | bytes 245776 | tf_op jit(solution)/shard_map/reduce_scatter | solution.py:43
  413.8 19.3 %all_gather.55 = bf16[640,768]{1,0:T(8,128)(2,1)S(1)} all-gather(bf16[160,768]{1,0:T(8,128)(2,1)S(1)} %bitcast.234), channel_id=1, replica_groups=mesh['expert'=2,'shard'=4,'dp'=4] {'shard'}, dimensions={0}, use_global_device_ids=true | all-gather | bytes 1228800 | tf_op jit(solution)/shard_map/all_gather | solution.py:39
  443.5 19.4 %reduce-scatter.31.cloned.1.call-done = bf16[160,768]{1,0:T(8,128)(2,1)} async-done(((bf16[640,768]{1,0:T(8,128)(2,1)}), bf16[160,768]{1,0:T(8,128)(2,1)}) %reduce-scatter.31.cloned.1.call-update) | async-done | bytes 245776 | tf_op jit(solution)/shard_map/reduce_scatter | solution.py:43
  498.4 20.3 %reduce-scatter.51.cloned.1.call-done = bf16[48,2]{1,0:T(8,128)(2,1)} async-done(((bf16[768,2]{1,0:T(8,128)(2,1)}), bf16[48,2]{1,0:T(8,128)(2,1)}) %reduce-scatter.51.cloned.1.call-update) | async-done | bytes 208
  526.1 48.6 %reduce-scatter.49.cloned.1.call-done = bf16[48,2]{1,0:T(8,128)(2,1)} async-done(((bf16[768,2]{1,0:T(8,128)(2,1)}), bf16[48,2]{1,0:T(8,128)(2,1)}) %reduce-scatter.49.cloned.1.call-update) | async-done | bytes 208
  575.5 55.4 %reduce-scatter.55.cloned.1.call-done = bf16[48,2]{1,0:T(8,128)(2,1)} async-done(((bf16[768,2]{1,0:T(8,128)(2,1)}), bf16[48,2]{1,0:T(8,128)(2,1)}) %reduce-scatter.55.cloned.1.call-update) | async-done | bytes 208
  643.9 40.3 %psum.71 = f32[32,12]{0,1:T(8,128)} all-reduce(f32[32,12]{0,1:T(8,128)S(1)} %fusion.104), channel_id=1, replica_groups=mesh['expert'=2,'shard'=4,'dp'=4] {'expert','shard','dp'}, use_global_device_ids=true, to_apply=%region_58.59 | all-reduce | flops 384 | bytes 3072 | tf_op jit(solution)/shard_map/psum | solution.py:344
  692.2 61.3 %reduce-scatter.37.cloned.1.call-done = bf16[48,768]{1,0:T(8,128)(2,1)} async-done(((bf16[768,768]{1,0:T(8,128)(2,1)}), bf16[48,768]{1,0:T(8,128)(2,1)}) %reduce-scatter.37.cloned.1.call-update) | async-done | bytes 73744 | tf_op jit(solution)/shard_map/reduce_scatter | solution.py:313
  753.5 70.8 %reduce-scatter.35.cloned.1.call-done = bf16[48,2304]{1,0:T(8,128)(2,1)} async-done(((bf16[768,2304]{1,0:T(8,128)(2,1)}), bf16[48,2304]{1,0:T(8,128)(2,1)}) %reduce-scatter.35.cloned.1.call-update) | async-done | bytes 221200 | tf_op jit(solution)/shard_map/reduce_scatter | solution.py:310
  824.3 70.6 %reduce-scatter.33.cloned.1.call-done = bf16[48,2304]{1,0:T(8,128)(2,1)} async-done(((bf16[768,2304]{1,0:T(8,128)(2,1)}), bf16[48,2304]{1,0:T(8,128)(2,1)}) %reduce-scatter.33.cloned.1.call-update) | async-done | bytes 221200 | tf_op jit(solution)/shard_map/reduce_scatter | solution.py:310
  895.9 55.5 %reduce-scatter.53.cloned.1.call-done = bf16[48,2]{1,0:T(8,128)(2,1)} async-done(((bf16[768,2]{1,0:T(8,128)(2,1)}), bf16[48,2]{1,0:T(8,128)(2,1)}) %reduce-scatter.53.cloned.1.call-update) | async-done | bytes 208
  957.7 20.9 %reduce-scatter.43.cloned.1.call-done = bf16[192,768]{1,0:T(8,128)(2,1)} async-done(((bf16[768,768]{1,0:T(8,128)(2,1)}), bf16[192,768]{1,0:T(8,128)(2,1)}) %reduce-scatter.43.cloned.1.call-update) | async-done | bytes 294928 | tf_op jit(solution)/shard_map/reduce_scatter | solution.py:330
  978.6 28.3 %reduce-scatter.41.cloned.1.call-done = bf16[192,768]{1,0:T(8,128)(2,1)} async-done(((bf16[768,768]{1,0:T(8,128)(2,1)}), bf16[192,768]{1,0:T(8,128)(2,1)}) %reduce-scatter.41.cloned.1.call-update) | async-done | bytes 294928 | tf_op jit(solution)/shard_map/reduce_scatter | solution.py:330
  1009.1 26.2 %reduce-scatter.47.cloned.1.call-done = bf16[192,768]{1,0:T(8,128)(2,1)} async-done(((bf16[768,768]{1,0:T(8,128)(2,1)}), bf16[192,768]{1,0:T(8,128)(2,1)}) %reduce-scatter.47.cloned.1.call-update) | async-done | bytes 294928 | tf_op jit(solution)/shard_map/reduce_scatter | solution.py:333
  1035.2 28.3 %reduce-scatter.45.cloned.1.call-done = bf16[192,768]{1,0:T(8,128)(2,1)} async-done(((bf16[768,768]{1,0:T(8,128)(2,1)}), bf16[192,768]{1,0:T(8,128)(2,1)}) %reduce-scatter.45.cloned.1.call-update) | async-done | bytes 294928 | tf_op jit(solution)/shard_map/reduce_scatter | solution.py:333
  1065.7 31.0 %all-reduce.9.cloned.1.call-done = (bf16[1,48,2304]{2,1,0:T(8,128)(2,1)}, bf16[1,48,2304]{2,1,0:T(8,128)(2,1)}, bf16[1,48,768]{2,1,0:T(8,128)(2,1)}, bf16[1,48,768]{2,1,0:T(8,128)(2,1)}) async-done(((bf16[1,48,2304]{2,1,0:T(8,128)(2,1)}, bf16[1,48,2304]{2,1,0:T(8,128)(2,1)}, bf16[1,48,768]{2,1,0:T(8,128)(2,1)}, bf16[1,48,768]{2,1,0:T(8,128)(2,1)}), (bf16[1,48,2304]{2,1,0:T(8,128)(2,1)}, ...) | async-done | bytes 589840 | tf_op jit(solution)/shard_map/psum | solution.py:324
  (436 shorter events, 270.1 us)
Async XLA Ops:
  7.2 54.2 %all-gather.13.cloned.1.call-start = ((), (), s32[]{:S(2)}) async-start(), calls=%async_computation.36 | async-start | bytes 3760128 | tf_op jit(solution)/shard_map/all_gather | solution.py:50
  9.1 92.5 %all-gather.15.cloned.1.call-start = ((), (), s32[]{:S(2)}) async-start(), calls=%async_computation.37 | async-start | bytes 1253376 | tf_op jit(solution)/shard_map/all_gather | solution.py:51
  10.8 172.7 %reduce-scatter.25.cloned.1.call-start = ((), (), s32[]{:S(2)}) async-start(), calls=%async_computation.24 | async-start | bytes 1228800 | tf_op jit(solution)/shard_map/reduce_scatter | solution.py:43
  138.2 74.0 %all-gather.17.cloned.1.call-start = ((), (), s32[]{:S(2)}) async-start(), calls=%async_computation.38 | async-start | bytes 3760128 | tf_op jit(solution)/shard_map/all_gather | solution.py:50
  138.8 113.7 %all-gather.19.cloned.1.call-start = ((), (), s32[]{:S(2)}) async-start(), calls=%async_computation.39 | async-start | bytes 1253376 | tf_op jit(solution)/shard_map/all_gather | solution.py:51
  183.5 9.2 all-to-all-start.1
  187.0 126.7 %reduce-scatter.27.cloned.1.call-start = ((), (), s32[]{:S(2)}) async-start(), calls=%async_computation.25 | async-start | bytes 1228800 | tf_op jit(solution)/shard_map/reduce_scatter | solution.py:43
  313.6 8.5 all-to-all-start.3
  317.1 68.7 %reduce-scatter.29.cloned.1.call-start = ((), (), s32[]{:S(2)}) async-start(), calls=%async_computation.26 | async-start | bytes 1228800 | tf_op jit(solution)/shard_map/reduce_scatter | solution.py:43
  360.8 102.2 %reduce-scatter.31.cloned.1.call-start = ((), (), s32[]{:S(2)}) async-start(), calls=%async_computation.27 | async-start | bytes 1228800 | tf_op jit(solution)/shard_map/reduce_scatter | solution.py:43
  438.1 80.6 %reduce-scatter.51.cloned.1.call-start = ((), (), s32[]{:S(2)}) async-start(), calls=%async_computation.41 | async-start | bytes 208896
  439.5 135.2 %reduce-scatter.49.cloned.1.call-start = ((), (), s32[]{:S(2)}) async-start(), calls=%async_computation.40 | async-start | bytes 208896
  441.0 189.9 %reduce-scatter.55.cloned.1.call-start = ((), (), s32[]{:S(2)}) async-start(), calls=%async_computation.43 | async-start | bytes 208896
  441.9 250.2 %reduce-scatter.39.cloned.1.call-start = ((), (), s32[]{:S(2)}) async-start(), calls=%async_computation.31 | async-start | bytes 1253376 | tf_op jit(solution)/shard_map/reduce_scatter | solution.py:313
  443.5 310.0 %reduce-scatter.37.cloned.1.call-start = ((), (), s32[]{:S(2)}) async-start(), calls=%async_computation.30 | async-start | bytes 1253376 | tf_op jit(solution)/shard_map/reduce_scatter | solution.py:313
  475.1 349.2 %reduce-scatter.35.cloned.1.call-start = ((), (), s32[]{:S(2)}) async-start(), calls=%async_computation.29 | async-start | bytes 3760128 | tf_op jit(solution)/shard_map/reduce_scatter | solution.py:310
  478.2 416.7 %reduce-scatter.33.cloned.1.call-start = ((), (), s32[]{:S(2)}) async-start(), calls=%async_computation.28 | async-start | bytes 3760128 | tf_op jit(solution)/shard_map/reduce_scatter | solution.py:310
  485.3 466.1 %reduce-scatter.53.cloned.1.call-start = ((), (), s32[]{:S(2)}) async-start(), calls=%async_computation.42 | async-start | bytes 208896
  491.3 487.3 %reduce-scatter.43.cloned.1.call-start = ((), (), s32[]{:S(2)}) async-start(), calls=%async_computation.33 | async-start | bytes 1474560 | tf_op jit(solution)/shard_map/reduce_scatter | solution.py:330
  494.8 512.1 %reduce-scatter.41.cloned.1.call-start = ((), (), s32[]{:S(2)}) async-start(), calls=%async_computation.32 | async-start | bytes 1474560 | tf_op jit(solution)/shard_map/reduce_scatter | solution.py:330
  498.3 536.9 %reduce-scatter.47.cloned.1.call-start = ((), (), s32[]{:S(2)}) async-start(), calls=%async_computation.35 | async-start | bytes 1474560 | tf_op jit(solution)/shard_map/reduce_scatter | solution.py:333
  523.4 540.2 %reduce-scatter.45.cloned.1.call-start = ((), (), s32[]{:S(2)}) async-start(), calls=%async_computation.34 | async-start | bytes 1474560 | tf_op jit(solution)/shard_map/reduce_scatter | solution.py:333
  635.8 460.8 %all-reduce.9.cloned.1.call-start = ((), (), s32[]{:S(2)}) async-start(), calls=%async_computation.44 | async-start | bytes 1179648 | tf_op jit(solution)/shard_map/psum | solution.py:324
  643.0 251.9 %copy-start.40 = (f32[128,768]{1,0:T(8,128)S(1)}, f32[128,768]{1,0:T(8,128)}, u32[]{:S(2)}) copy-start(f32[128,768]{1,0:T(8,128)} %get-tuple-element.76) | copy-start | bytes 1179652
  (112 other events, 2196.7 us)
Sparse Core Ops, SparseCore 0:
  10.9 50.4 all-gather.12
  64.2 37.3 all-gather.14
  138.4 24.3 reduce-scatter.24
  165.8 46.3 all-gather.16
  215.2 37.3 all-gather.18
  289.2 24.3 reduce-scatter.26
  360.9 24.8 reduce-scatter.28
  438.2 24.7 reduce-scatter.30
  466.5 52.1 reduce-scatter.50
  522.0 52.6 reduce-scatter.48
  578.2 52.6 reduce-scatter.54
  634.9 57.2 reduce-scatter.38
  696.3 57.0 reduce-scatter.36
  757.2 67.0 reduce-scatter.34
  828.0 66.8 reduce-scatter.32
  898.8 52.4 reduce-scatter.52
  953.8 24.7 reduce-scatter.42
  981.2 25.6 reduce-scatter.40
  1009.5 25.7 reduce-scatter.46
  1037.8 25.6 reduce-scatter.44
  1066.0 30.6 all-reduce.8
where the time goes:
time: 1120 us; the launch traced here: 1110 us
  waiting for transfers between devices  685 us (61%)
  blocking collectives  263 us (23%)
  matrix products  70.5 us (6%)
  local copies, waits for them, and re-layouts  43 us (4%)
  other arithmetic  22 us (2%)
  between operations  16.2 us (1%)
    unnamed x25, waiting for transfers between devices  181 us
    reduce_scatter x2, waiting for transfers between devices, body(): lax.psum_scatter(grad_proj.astype(jnp.bfloat16), ('shard', 'dp'), scatter...  141 us
    all_gather x4, blocking collectives, spread_rows(): return lax.all_gather(arrived, 'shard', axis=0, tiled=True)  80.6 us
    all_gather x2, waiting for transfers between devices, fetch_mixer(): lax.all_gather(collector[layer], ('shard', 'dp'), axis=0, tiled=True)  69.2 us
    reduce_scatter x2, waiting for transfers between devices, body(): lax.psum_scatter(grad_collect.astype(jnp.bfloat16), ('shard', 'dp'), scat...  69.2 us
    reduce_scatter x2, waiting for transfers between devices, body(): lax.psum_scatter(grad_down_t.astype(jnp.bfloat16), 'dp', scatter_dimensio...  54.5 us
    reduce_scatter x2, waiting for transfers between devices, body(): lax.psum_scatter(grad_up.astype(jnp.bfloat16), 'dp', scatter_dimension=0,...  49.2 us
    reduce_scatter x4, waiting for transfers between devices, sum_hidden(): lax.psum_scatter(partial_value.astype(jnp.bfloat16), 'shard', scatter_dim...  46.4 us
  transfers between devices with their start and end apart: 23, of which 22 were waited for; matrix products, arithmetic and copies ran while one was open for 8% of the time, Pallas kernels for 0%

commit v1 on v0

--- a/solution.py
+++ b/solution.py
@@ -45,22 +45,90 @@
     ).astype(jnp.float32)
 
 
+def pair_moves(axis_size, stride, count, shift):
+    moves = []
+    for place in range(axis_size):
+        part = (place // stride) % count
+        moves.append((place, place + ((part + shift) % count - part) * stride))
+    return moves
+
+
+def scatter_sum(parts, axis, stride, count):
+    axis_size = lax.axis_size(axis)
+    mine = (lax.axis_index(axis) // stride) % count
+    total = lax.dynamic_index_in_dim(parts, mine, 0, keepdims=False).astype(jnp.float32)
+    for shift in range(1, count):
+        leaving = lax.dynamic_index_in_dim(parts, (mine + shift) % count, 0, keepdims=False)
+        total = total + lax.ppermute(
+            leaving, axis, pair_moves(axis_size, stride, count, shift)
+        ).astype(jnp.float32)
+    return total.astype(jnp.bfloat16)
+
+
+def dp_levels():
+    size = lax.axis_size("dp")
+    low = 2 if size % 2 == 0 else 1
+    return size // low, low
+
+
+def reduce_experts(grad_up, grad_down_t):
+    high, low = dp_levels()
+    rows, columns = grad_up.shape
+    both = jnp.stack([grad_up.astype(jnp.bfloat16), grad_down_t.astype(jnp.bfloat16)])
+    both = both.reshape(2, high, low, rows // (high * low), columns)
+    part = scatter_sum(jnp.moveaxis(both, 2, 0), "dp", 1, low)
+    part = scatter_sum(jnp.moveaxis(part, 1, 0), "dp", low, high)
+    return part[0].astype(jnp.float32), part[1].astype(jnp.float32)
+
+
+def reduce_mixer(grads):
+    high, low = dp_levels()
+    owners, experts = lax.axis_size("shard"), lax.axis_size("expert")
+    widths = [grad.shape[1] for grad in grads]
+    unit = 128 * experts
+    spare = -sum(widths) % unit
+    rows = grads[0].shape[0]
+    packed = jnp.concatenate(
+        [grad.astype(jnp.bfloat16) for grad in grads] + [jnp.zeros((rows, spare), jnp.bfloat16)],
+        axis=1,
+    )
+    block = rows // (owners * high * low)
+    chunk = packed.shape[1] // experts
+    packed = packed.reshape(owners, high, low, block, packed.shape[1])
+    part = scatter_sum(jnp.moveaxis(packed, 2, 0), "dp", 1, low)
+    part = jnp.stack([part[..., at * chunk : (at + 1) * chunk] for at in range(experts)])
+    part = scatter_sum(part, "expert", 1, experts)
+    part = scatter_sum(jnp.moveaxis(part, 1, 0), "dp", low, high)
+    part = scatter_sum(part, "shard", 1, owners)
+    if experts == 2:
+        other = lax.ppermute(part, "expert", pair_moves(2, 1, 2, 1))
+        first = lax.axis_index("expert") == 0
+        whole = jnp.concatenate(
+            [jnp.where(first, part, other), jnp.where(first, other, part)], axis=1
+        )
+    else:
+        whole = lax.all_gather(part, "expert", axis=1, tiled=True)
+    whole = whole.astype(jnp.float32)
+    shares, start = [], 0
+    for width in widths:
+        shares.append(whole[:, start : start + width])
+        start += width
+    return shares
+
+
 def fetch_mixer(projection, collector, router, scales, layer):
-    return (
-        lax.all_gather(projection[layer], ("shard", "dp"), axis=0, tiled=True),
-        lax.all_gather(collector[layer], ("shard", "dp"), axis=0, tiled=True),
-        lax.all_gather(router[layer], ("shard", "dp"), axis=0, tiled=True),
-        lax.all_gather(scales[layer], ("shard", "dp"), axis=0, tiled=True),
-    )
-
-
-def fetch_again(projection, collector, router, scales, layer):
-    return (
-        lax.all_gather(projection[layer], ("shard", "dp"), axis=0, tiled=True),
-        lax.all_gather(collector[layer], ("shard", "dp"), axis=0, tiled=True),
-        lax.all_gather(router[layer], ("shard", "dp"), axis=0, tiled=True),
-        lax.all_gather(scales[layer], ("shard", "dp"), axis=0, tiled=True),
-    )
+    pieces = (projection[layer], collector[layer], router[layer], scales[layer])
+    widths = [piece.shape[1] for piece in pieces]
+    spare = -sum(widths) % 128
+    packed = jnp.concatenate(
+        pieces + (jnp.zeros((pieces[0].shape[0], spare), jnp.bfloat16),), axis=1
+    )
+    whole = lax.all_gather(packed, ("shard", "dp"), axis=0, tiled=True)
+    fetched, start = [], 0
+    for width in widths:
+        fetched.append(whole[:, start : start + width])
+        start += width
+    return tuple(fetched)
 
 
 def score_heads(queries, key_heads, bias_heads, same_segment):
@@ -131,8 +199,11 @@
     route_float = route_hot.astype(jnp.float32)
     residual = tokens.astype(jnp.float32)
     stored = []
+    gathered = [
+        fetch_mixer(projection, collector, router, scales, layer) for layer in range(layers)
+    ]
     for layer in range(layers):
-        fetched = fetch_mixer(projection, collector, router, scales, layer)
+        fetched = gathered[layer]
         proj_full, collect_full, router_full, scales_full = fetched
         gain_one = scales_full[:, 0].astype(jnp.float32)
         gain_two = scales_full[:, 1].astype(jnp.float32)
@@ -210,9 +281,7 @@
     )
     for layer in reversed(range(layers)):
         saved_layer = stored[layer]
-        proj_full, collect_full, router_full, scales_full = fetch_again(
-            projection, collector, router, scales, layer
-        )
+        proj_full, collect_full, router_full, scales_full = saved_layer["fetched"]
         gain_one = scales_full[:, 0].astype(jnp.float32)
         gain_two = scales_full[:, 1].astype(jnp.float32)
         router_float = router_full.astype(jnp.float32)
@@ -306,34 +375,8 @@
         )
         grad_residual = grad_middle + grad_in_norm
         grad_scales = jnp.stack([grad_gain_one, grad_gain_two], axis=1)
-        shares = (
-            lax.psum_scatter(
-                grad_proj.astype(jnp.bfloat16), ("shard", "dp"), scatter_dimension=0, tiled=True
-            ).astype(jnp.float32),
-            lax.psum_scatter(
-                grad_collect.astype(jnp.bfloat16), ("shard", "dp"), scatter_dimension=0, tiled=True
-            ).astype(jnp.float32),
-            lax.psum_scatter(
-                grad_router.astype(jnp.bfloat16), ("shard", "dp"), scatter_dimension=0, tiled=True
-            ).astype(jnp.float32),
-            lax.psum_scatter(
-                grad_scales.astype(jnp.bfloat16), ("shard", "dp"), scatter_dimension=0, tiled=True
-            ).astype(jnp.float32),
-        )
-        shares = (
-            lax.psum(shares[0].astype(jnp.bfloat16), "expert").astype(jnp.float32),
-            lax.psum(shares[1].astype(jnp.bfloat16), "expert").astype(jnp.float32),
-            lax.psum(shares[2].astype(jnp.bfloat16), "expert").astype(jnp.float32),
-            lax.psum(shares[3].astype(jnp.bfloat16), "expert").astype(jnp.float32),
-        )
-        expert_shares = (
-            lax.psum_scatter(
-                grad_up.astype(jnp.bfloat16), "dp", scatter_dimension=0, tiled=True
-            ).astype(jnp.float32),
-            lax.psum_scatter(
-                grad_down_t.astype(jnp.bfloat16), "dp", scatter_dimension=0, tiled=True
-            ).astype(jnp.float32),
-        )
+        expert_shares = reduce_experts(grad_up, grad_down_t)
+        shares = reduce_mixer([grad_proj, grad_collect, grad_router, grad_scales])
         proj_grads.insert(0, shares[0])
         collect_grads.insert(0, shares[1])
         router_grads.insert(0, shares[2])

time: 1120 us -> 652 us (0.58)
  waiting for transfers between devices: 685 us -> 216 us
  blocking collectives: 263 us -> 189 us
  local copies, waits for them, and re-layouts: 43 us -> 71.1 us
  starting transfers between devices: 8.35 us -> 35.5 us
  other arithmetic: 22 us -> 36 us
    reduce_scatter x8 -> x0, waiting for transfers between devices: 314 us -> none  [the longest x2 141 us: body(): lax.psum_scatter(grad_proj.astype(jnp.bfloat16), ('shard', 'dp'), scatter...]
    unnamed x25 -> x6, waiting for transfers between devices: 181 us -> 0.1 us
    all_gather x4 -> x0, blocking collectives: 88.3 us -> none  [the longest x2 44.5 us: fetch_mixer(): lax.all_gather(router[layer], ('shard', 'dp'), axis=0, tiled=True)]
    psum x1, blocking collectives: 40.3 us -> 85.4 us  [body(): table_sum = lax.psum(table_total, ('expert', 'shard', 'dp'))]
    ppermute x0 -> x18, waiting for transfers between devices: none -> 43.9 us  [the longest x16 39.6 us: scatter_sum(): lax.ppermute(leaving, axis, pair_moves(axis_size, stride, count, shift))]
    psum x1 -> x0, waiting for transfers between devices: 31 us -> none  [body(): lax.psum(shares[0].astype(jnp.bfloat16), 'expert').astype(jnp.float32)]
    concatenate x0 -> x4, local copies, waits for them, and re-layouts: none -> 18.8 us  [the longest x2 17.2 us: reduce_mixer(): jnp.concatenate([grad.astype(jnp.bfloat16) for grad in grads] + [jnp.zero...]
    all_to_all x2 -> x0, blocking collectives: 17.4 us -> none  [return_rows(): lax.all_to_all(buffer, 'expert', split_axis=0, concat_axis=0, tiled=True)]
  transfers between devices with their start and end apart: 23 -> 29, of which waited for: 22 -> 16; matrix products, arithmetic and copies ran while one was open for 8% -> 12% of each run, Pallas kernels for 0% -> 0%
where the time goes in v1:
time: 652 us; the launch traced here: 642 us
  waiting for transfers between devices  216 us (33%)
  blocking collectives  189 us (29%)
  matrix products  78.1 us (12%)
  local copies, waits for them, and re-layouts  71.1 us (11%)
  other arithmetic  36 us (6%)
  starting transfers between devices  35.5 us (5%)
  between operations  16.5 us (3%)
    all_gather x2, waiting for transfers between devices, fetch_mixer(): whole = lax.all_gather(packed, ('shard', 'dp'), axis=0, tiled=True)  101 us
    psum x1, blocking collectives, body(): table_sum = lax.psum(table_total, ('expert', 'shard', 'dp'))  85.4 us
    all_gather x4, blocking collectives, spread_rows(): return lax.all_gather(arrived, 'shard', axis=0, tiled=True)  79.7 us
    reduce_scatter x4, waiting for transfers between devices, sum_hidden(): lax.psum_scatter(partial_value.astype(jnp.bfloat16), 'shard', scatter_dim...  62.2 us
    ppermute x16, waiting for transfers between devices, scatter_sum(): lax.ppermute(leaving, axis, pair_moves(axis_size, stride, count, shift))  39.6 us
    all_to_all x3, blocking collectives, send_rows(): lax.all_to_all(buffer, 'expert', split_axis=0, concat_axis=0, tiled=True)  23.6 us
    unnamed x231, local copies, waits for them, and re-layouts  19.5 us
    concatenate x2, local copies, waits for them, and re-layouts, reduce_mixer(): jnp.concatenate([grad.astype(jnp.bfloat16) for grad in grads] + [jnp.zero...  17.2 us
  transfers between devices with their start and end apart: 29, of which 16 were waited for; matrix products, arithmetic and copies ran while one was open for 12% of the time, Pallas kernels for 0%

profile of v1, /device:TPU:0, one launch (start us, length us, event | category | flops | bytes accessed | tf_op | source)
XLA Modules:
  0.0 642.1 jit_solution(6810399390488483441)
XLA Ops:
  22.3 48.5 %all-gather.3.cloned.1.call-done = bf16[768,3200]{1,0:T(8,128)(2,1)} async-done(((bf16[48,3200]{1,0:T(8,128)(2,1)}), bf16[768,3200]{1,0:T(8,128)(2,1)}) %all-gather.3.cloned.1.call-update) | async-done | bytes 4915216 | tf_op jit(solution)/shard_map/all_gather | solution.py:126
  78.5 8.1 %all_to_all.40 = bf16[2,80,768]{2,1,0:T(8,128)(2,1)S(1)} all-to-all(bf16[2,80,768]{2,1,0:T(8,128)(2,1)S(1)} %bitcast.317), channel_id=1, replica_groups=mesh['expert'=2,'shard'=4,'dp'=4] {'expert'}, dimensions={0} | all-to-all | bytes 491520 | tf_op jit(solution)/shard_map/all_to_all | solution.py:31
  86.6 20.4 %all_gather.19 = bf16[640,768]{1,0:T(8,128)(2,1)S(1)} all-gather(bf16[160,768]{1,0:T(8,128)(2,1)S(1)} %bitcast.310), channel_id=1, replica_groups=mesh['expert'=2,'shard'=4,'dp'=4] {'shard'}, dimensions={0}, use_global_device_ids=true | all-gather | bytes 1228800 | tf_op jit(solution)/shard_map/all_gather | solution.py:39
  115.6 20.6 %reduce-scatter.5.cloned.1.call-done = bf16[160,768]{1,0:T(8,128)(2,1)} async-done(((bf16[640,768]{1,0:T(8,128)(2,1)}), bf16[160,768]{1,0:T(8,128)(2,1)}) %reduce-scatter.5.cloned.1.call-update) | async-done | bytes 245776 | tf_op jit(solution)/shard_map/reduce_scatter | solution.py:43
  139.9 52.4 %all-gather.5.cloned.1.call-done = bf16[768,3200]{1,0:T(8,128)(2,1)} async-done(((bf16[48,3200]{1,0:T(8,128)(2,1)}), bf16[768,3200]{1,0:T(8,128)(2,1)}) %all-gather.5.cloned.1.call-update) | async-done | bytes 4915216 | tf_op jit(solution)/shard_map/all_gather | solution.py:126
  204.4 8.1 %all_to_all.41 = bf16[2,80,768]{2,1,0:T(8,128)(2,1)S(1)} all-to-all(bf16[2,80,768]{2,1,0:T(8,128)(2,1)S(1)} %bitcast.318), channel_id=1, replica_groups=mesh['expert'=2,'shard'=4,'dp'=4] {'expert'}, dimensions={0} | all-to-all | bytes 491520 | tf_op jit(solution)/shard_map/all_to_all | solution.py:31
  212.5 20.4 %all_gather.21 = bf16[640,768]{1,0:T(8,128)(2,1)S(1)} all-gather(bf16[160,768]{1,0:T(8,128)(2,1)S(1)} %bitcast.311), channel_id=1, replica_groups=mesh['expert'=2,'shard'=4,'dp'=4] {'shard'}, dimensions={0}, use_global_device_ids=true | all-gather | bytes 1228800 | tf_op jit(solution)/shard_map/all_gather | solution.py:39
  238.3 23.7 %reduce-scatter.7.cloned.1.call-done = bf16[160,768]{1,0:T(8,128)(2,1)} async-done(((bf16[640,768]{1,0:T(8,128)(2,1)}), bf16[160,768]{1,0:T(8,128)(2,1)}) %reduce-scatter.7.cloned.1.call-update) | async-done | bytes 245776 | tf_op jit(solution)/shard_map/reduce_scatter | solution.py:43
  274.0 7.5 %all_to_all.42 = bf16[2,80,768]{2,1,0:T(8,128)(2,1)S(1)} all-to-all(bf16[2,80,768]{2,1,0:T(8,128)(2,1)S(1)} %bitcast.335), channel_id=1, replica_groups=mesh['expert'=2,'shard'=4,'dp'=4] {'expert'}, dimensions={0} | all-to-all | bytes 491520 | tf_op jit(solution)/shard_map/all_to_all | solution.py:31
  281.4 19.4 %all_gather.22 = bf16[640,768]{1,0:T(8,128)(2,1)S(1)} all-gather(bf16[160,768]{1,0:T(8,128)(2,1)S(1)} %bitcast.312), channel_id=1, replica_groups=mesh['expert'=2,'shard'=4,'dp'=4] {'shard'}, dimensions={0}, use_global_device_ids=true | all-gather | bytes 1228800 | tf_op jit(solution)/shard_map/all_gather | solution.py:39
  310.4 4.1 convolution_convert_fusion.6
  314.6 17.9 %reduce-scatter.9.cloned.1.call-done = bf16[160,768]{1,0:T(8,128)(2,1)} async-done(((bf16[640,768]{1,0:T(8,128)(2,1)}), bf16[160,768]{1,0:T(8,128)(2,1)}) %reduce-scatter.9.cloned.1.call-update) | async-done | bytes 245776 | tf_op jit(solution)/shard_map/reduce_scatter | solution.py:43
  332.4 4.5 all-to-all-start.5
  367.7 19.5 %all_gather.23 = bf16[640,768]{1,0:T(8,128)(2,1)S(1)} all-gather(bf16[160,768]{1,0:T(8,128)(2,1)S(1)} %bitcast.309), channel_id=1, replica_groups=mesh['expert'=2,'shard'=4,'dp'=4] {'shard'}, dimensions={0}, use_global_device_ids=true | all-gather | bytes 1228800 | tf_op jit(solution)/shard_map/all_gather | solution.py:39
  420.4 8.7 %concatenate.36 = bf16[768,3328]{1,0:T(8,128)(2,1)} concatenate(bf16[768,2304]{1,0:T(8,128)(2,1)} %convolution_convert_fusion, bf16[768,768]{1,0:T(8,128)(2,1)} %convolution_convert_fusion.4, bf16[768,2]{1,0:T(8,128)(2,1)} %copy.187, bf16[768,1]{1,0:T(8,128)(2,1)} %stack.138, bf16[768,1]{1,0:T(8,128)(2,1)} %stack.139, bf16[768,252]{1,0:T(8,128)(2,1)S(1)} %broadcast.259), dimensions={1} | concatenate | bytes 10223616 | tf_op jit(solution)/shard_map/concatenate | solution.py:91
  430.5 6.7 %collective-permute-done.17 = bf16[2,192,768]{2,1,0:T(8,128)(2,1)} collective-permute-done((bf16[2,192,768]{2,1,0:T(8,128)(2,1)}, bf16[2,192,768]{2,1,0:T(8,128)(2,1)}, u32[]{:S(2)}, u32[]{:S(2)}) %collective-permute-start.17) | collective-permute-done | bytes 589856 | tf_op jit(solution)/shard_map/ppermute | solution.py:62
  458.5 4.0 fusion.89
  465.2 8.5 %concatenate.34 = bf16[768,3328]{1,0:T(8,128)(2,1)} concatenate(bf16[768,2304]{1,0:T(8,128)(2,1)} %convolution_convert_fusion.1, bf16[768,768]{1,0:T(8,128)(2,1)S(1)} %convolution_convert_fusion.5, bf16[768,2]{1,0:T(8,128)(2,1)S(1)} %copy-done.40, bf16[768,1]{1,0:T(8,128)(2,1)S(1)} %stack.136, bf16[768,1]{1,0:T(8,128)(2,1)S(1)} %stack.137, bf16[768,252]{1,0:T(8,128)(2,1)S(1)} %broadcast.259), dimensions={1} | concatenate | bytes 10223616 | tf_op jit(solution)/shard_map/concatenate | solution.py:91
  473.7 4.6 constant_dynamic-slice_fusion.1
  491.8 85.4 %psum.7 = f32[32,12]{0,1:T(8,128)} all-reduce(f32[32,12]{0,1:T(8,128)S(1)} %fusion.130), channel_id=1, replica_groups=mesh['expert'=2,'shard'=4,'dp'=4] {'expert','shard','dp'}, use_global_device_ids=true, to_apply=%region_38.39 | all-reduce | flops 384 | bytes 3072 | tf_op jit(solution)/shard_map/psum | solution.py:387
  586.1 13.2 %collective-permute-done.2 = bf16[4,48,1664]{2,1,0:T(8,128)(2,1)S(1)} collective-permute-done((bf16[4,48,1664]{2,1,0:T(8,128)(2,1)S(1)}, bf16[4,48,1664]{2,1,0:T(8,128)(2,1)S(1)}, u32[]{:S(2)}, u32[]{:S(2)}) %collective-permute-start.2) | collective-permute-done | bytes 639008 | tf_op jit(solution)/shard_map/ppermute | solution.py:62
  603.4 7.3 %collective-permute-done.9 = bf16[4,48,1664]{2,1,0:T(8,128)(2,1)S(1)} collective-permute-done((bf16[4,48,1664]{2,1,0:T(8,128)(2,1)S(1)}, bf16[4,48,1664]{2,1,0:T(8,128)(2,1)S(1)}, u32[]{:S(2)}, u32[]{:S(2)}) %collective-permute-start.9) | collective-permute-done | bytes 639008 | tf_op jit(solution)/shard_map/ppermute | solution.py:62
  620.0 5.9 collective-permute-done.11
  627.1 4.3 collective-permute-done.13
  (462 shorter events, 202.0 us)
Async XLA Ops:
  7.2 63.6 %all-gather.3.cloned.1.call-start = ((), (), s32[]{:S(2)}) async-start(), calls=%async_computation.12 | async-start | bytes 5222400 | tf_op jit(solution)/shard_map/all_gather | solution.py:126
  13.5 122.7 %reduce-scatter.5.cloned.1.call-start = ((), (), s32[]{:S(2)}) async-start(), calls=%async_computation.13 | async-start | bytes 1228800 | tf_op jit(solution)/shard_map/reduce_scatter | solution.py:43
  112.5 79.8 %all-gather.5.cloned.1.call-start = ((), (), s32[]{:S(2)}) async-start(), calls=%async_computation.14 | async-start | bytes 5222400 | tf_op jit(solution)/shard_map/all_gather | solution.py:126
  136.2 58.0 %all-to-all-start.1 = ((bf16[2,80,768]{2,1,0:T(8,128)(2,1)}), bf16[2,80,768]{2,1,0:T(8,128)(2,1)S(1)}, u32[]{:S(2)}, u32[]{:S(2)}) async-start(bf16[2,80,768]{2,1,0:T(8,128)(2,1)} %bitcast.333), calls=%async_computation.2 | async-start | bytes 491520 | tf_op jit(solution)/shard_map/all_to_all | solution.py:35
  139.7 122.3 %reduce-scatter.7.cloned.1.call-start = ((), (), s32[]{:S(2)}) async-start(), calls=%async_computation.15 | async-start | bytes 1228800 | tf_op jit(solution)/shard_map/reduce_scatter | solution.py:43
  265.5 67.0 %reduce-scatter.9.cloned.1.call-start = ((), (), s32[]{:S(2)}) async-start(), calls=%async_computation.16 | async-start | bytes 1228800 | tf_op jit(solution)/shard_map/reduce_scatter | solution.py:43
  332.4 9.7 %all-to-all-start.5 = ((bf16[2,80,768]{2,1,0:T(8,128)(2,1)}), bf16[2,80,768]{2,1,0:T(8,128)(2,1)}, u32[]{:S(2)}, u32[]{:S(2)}) async-start(bf16[2,80,768]{2,1,0:T(8,128)(2,1)} %bitcast.331), calls=%async_computation.8 | async-start | bytes 491520 | tf_op jit(solution)/shard_map/all_to_all | solution.py:35
  356.7 11.0 %all-to-all-start.6 = ((bf16[2,80,768]{2,1,0:T(8,128)(2,1)}), bf16[2,80,768]{2,1,0:T(8,128)(2,1)S(1)}, u32[]{:S(2)}, u32[]{:S(2)}) async-start(bf16[2,80,768]{2,1,0:T(8,128)(2,1)} %bitcast.316), calls=%async_computation.9 | async-start | bytes 491520 | tf_op jit(solution)/shard_map/all_to_all | solution.py:31
  360.2 79.3 %reduce-scatter.11.cloned.1.call-start = ((), (), s32[]{:S(2)}) async-start(), calls=%async_computation.17 | async-start | bytes 1228800 | tf_op jit(solution)/shard_map/reduce_scatter | solution.py:43
  396.8 9.5 %collective-permute-start.14 = (bf16[2,2,192,768]{3,2,0,1:T(8,128)(2,1)}, bf16[2,2,192,768]{3,2,0,1:T(8,128)(2,1)}, u32[]{:S(2)}, u32[]{:S(2)}) collective-permute-start(bf16[2,2,192,768]{3,2,0,1:T(8,128)(2,1)} %bitcast.274), channel_id=1, source_target_pairs={{0,1},{1,0},{2,3},{3,2},{4,5},{5,4},{6,7},{7,6},{8,9},{9,8},{10,11... | collective-permute-start | bytes 3538952 | tf_op jit(solution)/shard_map/ppermute | solution.py:62
  399.4 11.2 %collective-permute-start.16 = (bf16[2,2,192,768]{3,2,0,1:T(8,128)(2,1)}, bf16[2,2,192,768]{3,2,0,1:T(8,128)(2,1)}, u32[]{:S(2)}, u32[]{:S(2)}) collective-permute-start(bf16[2,2,192,768]{3,2,0,1:T(8,128)(2,1)} %bitcast.273), channel_id=1, source_target_pairs={{0,1},{1,0},{2,3},{3,2},{4,5},{5,4},{6,7},{7,6},{8,9},{9,8},{10,11... | collective-permute-start | bytes 3538952 | tf_op jit(solution)/shard_map/ppermute | solution.py:62
  408.9 20.2 %collective-permute-start.15 = (bf16[2,192,768]{2,1,0:T(8,128)(2,1)}, bf16[2,192,768]{2,1,0:T(8,128)(2,1)}, u32[]{:S(2)}, u32[]{:S(2)}) collective-permute-start(bf16[2,192,768]{2,1,0:T(8,128)(2,1)} %dynamic-slice_bitcast_fusion.3), channel_id=1, source_target_pairs={{0,2},{1,3},{2,0},{3,1},{4,6},{5,7},{6,4},{7,5},{8,10},{9,11},{10,... | collective-permute-start | bytes 1769480 | tf_op jit(solution)/shard_map/ppermute | solution.py:62
  413.5 23.6 %collective-permute-start.17 = (bf16[2,192,768]{2,1,0:T(8,128)(2,1)}, bf16[2,192,768]{2,1,0:T(8,128)(2,1)}, u32[]{:S(2)}, u32[]{:S(2)}) collective-permute-start(bf16[2,192,768]{2,1,0:T(8,128)(2,1)} %dynamic-slice_bitcast_fusion.2), channel_id=1, source_target_pairs={{0,2},{1,3},{2,0},{3,1},{4,6},{5,7},{6,4},{7,5},{8,10},{9,11},{10,... | collective-permute-start | bytes 1769480 | tf_op jit(solution)/shard_map/ppermute | solution.py:62
  486.0 93.2 %collective-permute-start.1 = (bf16[4,2,48,1664]{3,2,0,1:T(8,128)(2,1)}, bf16[4,2,48,1664]{3,2,0,1:T(8,128)(2,1)}, u32[]{:S(2)}, u32[]{:S(2)}) collective-permute-start(bf16[4,2,48,1664]{3,2,0,1:T(8,128)(2,1)} %fusion.35), channel_id=1, source_target_pairs={{0,16},{16,0},{1,17},{17,1},{2,18},{18,2},{3,19},{19,3},{4,20},{20... | collective-permute-start | bytes 3833864 | tf_op jit(solution)/shard_map/ppermute | solution.py:62
  490.8 93.2 %collective-permute-start.8 = (bf16[4,2,48,1664]{3,2,0,1:T(8,128)(2,1)}, bf16[4,2,48,1664]{3,2,0,1:T(8,128)(2,1)}, u32[]{:S(2)}, u32[]{:S(2)}) collective-permute-start(bf16[4,2,48,1664]{3,2,0,1:T(8,128)(2,1)} %fusion.31), channel_id=1, source_target_pairs={{0,16},{16,0},{1,17},{17,1},{2,18},{18,2},{3,19},{19,3},{4,20},{20... | collective-permute-start | bytes 3833864 | tf_op jit(solution)/shard_map/ppermute | solution.py:62
  581.4 18.0 %collective-permute-start.2 = (bf16[4,48,1664]{2,1,0:T(8,128)(2,1)S(1)}, bf16[4,48,1664]{2,1,0:T(8,128)(2,1)S(1)}, u32[]{:S(2)}, u32[]{:S(2)}) collective-permute-start(bf16[4,48,1664]{2,1,0:T(8,128)(2,1)S(1)} %dynamic-slice_bitcast_fusion.1), channel_id=1, source_target_pairs={{0,2},{1,3},{2,0},{3,1},{4,6},{5,7},{6,4},{7,5},{8,10},{9,11},{10,... | collective-permute-start | bytes 1916936 | tf_op jit(solution)/shard_map/ppermute | solution.py:62
  586.0 24.7 %collective-permute-start.9 = (bf16[4,48,1664]{2,1,0:T(8,128)(2,1)S(1)}, bf16[4,48,1664]{2,1,0:T(8,128)(2,1)S(1)}, u32[]{:S(2)}, u32[]{:S(2)}) collective-permute-start(bf16[4,48,1664]{2,1,0:T(8,128)(2,1)S(1)} %dynamic-slice_bitcast_fusion), channel_id=1, source_target_pairs={{0,2},{1,3},{2,0},{3,1},{4,6},{5,7},{6,4},{7,5},{8,10},{9,11},{10,... | collective-permute-start | bytes 1916936 | tf_op jit(solution)/shard_map/ppermute | solution.py:62
  599.5 15.3 %collective-permute-start.3 = (bf16[48,1664]{1,0:T(8,128)(2,1)S(1)}, bf16[48,1664]{1,0:T(8,128)(2,1)S(1)}, u32[]{:S(2)}, u32[]{:S(2)}) collective-permute-start(bf16[48,1664]{1,0:T(8,128)(2,1)S(1)} %get-tuple-element.42), channel_id=1, source_target_pairs={{0,4},{4,8},{8,12},{12,0},{1,5},{5,9},{9,13},{13,1},{2,6},{6,10},{... | collective-permute-start | bytes 479240 | tf_op jit(solution)/shard_map/ppermute | solution.py:62
  599.6 15.3 %collective-permute-start.5 = (bf16[48,1664]{1,0:T(8,128)(2,1)S(1)}, bf16[48,1664]{1,0:T(8,128)(2,1)S(1)}, u32[]{:S(2)}, u32[]{:S(2)}) collective-permute-start(bf16[48,1664]{1,0:T(8,128)(2,1)S(1)} %get-tuple-element.43), channel_id=1, source_target_pairs={{0,12},{4,0},{8,4},{12,8},{1,13},{5,1},{9,5},{13,9},{2,14},{6,2},{... | collective-permute-start | bytes 479240 | tf_op jit(solution)/shard_map/ppermute | solution.py:62
  603.4 11.5 %collective-permute-start.4 = (bf16[48,1664]{1,0:T(8,128)(2,1)S(1)}, bf16[48,1664]{1,0:T(8,128)(2,1)S(1)}, u32[]{:S(2)}, u32[]{:S(2)}) collective-permute-start(bf16[48,1664]{1,0:T(8,128)(2,1)S(1)} %get-tuple-element.44), channel_id=1, source_target_pairs={{0,8},{4,12},{8,0},{12,4},{1,9},{5,13},{9,1},{13,5},{2,10},{6,14},... | collective-permute-start | bytes 479240 | tf_op jit(solution)/shard_map/ppermute | solution.py:62
  611.0 9.0 %collective-permute-start.10 = (bf16[48,1664]{1,0:T(8,128)(2,1)S(1)}, bf16[48,1664]{1,0:T(8,128)(2,1)S(1)}, u32[]{:S(2)}, u32[]{:S(2)}) collective-permute-start(bf16[48,1664]{1,0:T(8,128)(2,1)S(1)} %get-tuple-element.45), channel_id=1, source_target_pairs={{0,4},{4,8},{8,12},{12,0},{1,5},{5,9},{9,13},{13,1},{2,6},{6,10},{... | collective-permute-start | bytes 479240 | tf_op jit(solution)/shard_map/ppermute | solution.py:62
  611.1 8.9 %collective-permute-start.12 = (bf16[48,1664]{1,0:T(8,128)(2,1)S(1)}, bf16[48,1664]{1,0:T(8,128)(2,1)S(1)}, u32[]{:S(2)}, u32[]{:S(2)}) collective-permute-start(bf16[48,1664]{1,0:T(8,128)(2,1)S(1)} %get-tuple-element.46), channel_id=1, source_target_pairs={{0,12},{4,0},{8,4},{12,8},{1,13},{5,1},{9,5},{13,9},{2,14},{6,2},{... | collective-permute-start | bytes 479240 | tf_op jit(solution)/shard_map/ppermute | solution.py:62
  614.9 11.0 %collective-permute-start.11 = (bf16[48,1664]{1,0:T(8,128)(2,1)S(1)}, bf16[48,1664]{1,0:T(8,128)(2,1)S(1)}, u32[]{:S(2)}, u32[]{:S(2)}) collective-permute-start(bf16[48,1664]{1,0:T(8,128)(2,1)S(1)} %get-tuple-element.47), channel_id=1, source_target_pairs={{0,8},{4,12},{8,0},{12,4},{1,9},{5,13},{9,1},{13,5},{2,10},{6,14},... | collective-permute-start | bytes 479240 | tf_op jit(solution)/shard_map/ppermute | solution.py:62
  615.0 11.9 %collective-permute-start.6 = (bf16[48,1664]{1,0:T(8,128)(2,1)S(1)}, bf16[48,1664]{1,0:T(8,128)(2,1)S(1)}, u32[]{:S(2)}, u32[]{:S(2)}) collective-permute-start(bf16[48,1664]{1,0:T(8,128)(2,1)S(1)} %fusion.104), channel_id=1, source_target_pairs={{0,16},{16,0},{1,17},{17,1},{2,18},{18,2},{3,19},{19,3},{4,20},{20... | collective-permute-start | bytes 479240 | tf_op jit(solution)/shard_map/ppermute | solution.py:104
  (117 other events, 1558.9 us)
Sparse Core Ops, SparseCore 0:
  13.6 57.1 all-gather.2
  112.6 23.5 reduce-scatter.4
  139.2 53.0 all-gather.4
  238.4 23.5 reduce-scatter.6
  307.7 24.7 reduce-scatter.8
  406.4 26.7 reduce-scatter.10

commit v2 on v1

--- a/solution.py
+++ b/solution.py
@@ -25,24 +25,6 @@
         grad_normed - normed * jnp.mean(grad_normed * normed, axis=-1, keepdims=True)
     )
     return (grad_inputs, grad_gain)
-
-
-def send_rows(buffer):
-    return lax.all_to_all(buffer, "expert", split_axis=0, concat_axis=0, tiled=True)
-
-
-def return_rows(buffer):
-    return lax.all_to_all(buffer, "expert", split_axis=0, concat_axis=0, tiled=True)
-
-
-def spread_rows(arrived):
-    return lax.all_gather(arrived, "shard", axis=0, tiled=True)
-
-
-def sum_hidden(partial_value):
-    return lax.psum_scatter(
-        partial_value.astype(jnp.bfloat16), "shard", scatter_dimension=0, tiled=True
-    ).astype(jnp.float32)
 
 
 def pair_moves(axis_size, stride, count, shift):
@@ -51,6 +33,39 @@
         part = (place // stride) % count
         moves.append((place, place + ((part + shift) % count - part) * stride))
     return moves
+
+
+def send_rows(parts):
+    experts, owners = lax.axis_size("expert"), lax.axis_size("shard")
+    mine = lax.axis_index("expert")
+    blocks = []
+    for away in range(experts):
+        piece = lax.dynamic_index_in_dim(parts, (mine + away) % experts, 0, keepdims=False)
+        if away:
+            piece = lax.ppermute(piece, "expert", pair_moves(experts, 1, experts, away))
+        blocks.append(piece)
+        for shift in range(1, owners):
+            blocks.append(lax.ppermute(piece, "shard", pair_moves(owners, 1, owners, shift)))
+    return jnp.concatenate(blocks)
+
+
+def return_rows(partial_value):
+    experts, owners = lax.axis_size("expert"), lax.axis_size("shard")
+    mine = lax.axis_index("expert")
+    parts = partial_value.astype(jnp.bfloat16)
+    parts = parts.reshape(experts, owners, -1, partial_value.shape[1])
+    result = jnp.zeros((experts,) + parts.shape[2:], jnp.bfloat16)
+    for away in reversed(range(experts)):
+        total = parts[away, 0].astype(jnp.float32)
+        for shift in range(1, owners):
+            total = total + lax.ppermute(
+                parts[away, shift], "shard", pair_moves(owners, 1, owners, owners - shift)
+            ).astype(jnp.float32)
+        total = total.astype(jnp.bfloat16)
+        if away:
+            total = lax.ppermute(total, "expert", pair_moves(experts, 1, experts, experts - away))
+        result = lax.dynamic_update_index_in_dim(result, total, (mine + away) % experts, 0)
+    return result.reshape(-1, partial_value.shape[1])
 
 
 def scatter_sum(parts, axis, stride, count):
@@ -81,20 +96,12 @@
     return part[0].astype(jnp.float32), part[1].astype(jnp.float32)
 
 
-def reduce_mixer(grads):
+def reduce_rows(grad):
     high, low = dp_levels()
     owners, experts = lax.axis_size("shard"), lax.axis_size("expert")
-    widths = [grad.shape[1] for grad in grads]
-    unit = 128 * experts
-    spare = -sum(widths) % unit
-    rows = grads[0].shape[0]
-    packed = jnp.concatenate(
-        [grad.astype(jnp.bfloat16) for grad in grads] + [jnp.zeros((rows, spare), jnp.bfloat16)],
-        axis=1,
-    )
-    block = rows // (owners * high * low)
-    chunk = packed.shape[1] // experts
-    packed = packed.reshape(owners, high, low, block, packed.shape[1])
+    block = grad.shape[0] // (owners * high * low)
+    chunk = grad.shape[1] // experts
+    packed = grad.astype(jnp.bfloat16).reshape(owners, high, low, block, grad.shape[1])
     part = scatter_sum(jnp.moveaxis(packed, 2, 0), "dp", 1, low)
     part = jnp.stack([part[..., at * chunk : (at + 1) * chunk] for at in range(experts)])
     part = scatter_sum(part, "expert", 1, experts)
@@ -108,27 +115,73 @@
         )
     else:
         whole = lax.all_gather(part, "expert", axis=1, tiled=True)
-    whole = whole.astype(jnp.float32)
-    shares, start = [], 0
-    for width in widths:
-        shares.append(whole[:, start : start + width])
-        start += width
-    return shares
-
-
-def fetch_mixer(projection, collector, router, scales, layer):
-    pieces = (projection[layer], collector[layer], router[layer], scales[layer])
-    widths = [piece.shape[1] for piece in pieces]
-    spare = -sum(widths) % 128
-    packed = jnp.concatenate(
-        pieces + (jnp.zeros((pieces[0].shape[0], spare), jnp.bfloat16),), axis=1
-    )
-    whole = lax.all_gather(packed, ("shard", "dp"), axis=0, tiled=True)
-    fetched, start = [], 0
-    for width in widths:
-        fetched.append(whole[:, start : start + width])
-        start += width
-    return tuple(fetched)
+    return whole.astype(jnp.float32)
+
+
+def sum_everywhere(value):
+    for axis in ("dp", "expert", "shard"):
+        size = lax.axis_size(axis)
+        if size & (size - 1):
+            value = lax.psum(value, axis)
+            continue
+        stride = 1
+        while stride < size:
+            value = value + lax.ppermute(value, axis, pair_moves(size, stride, 2, 1))
+            stride *= 2
+    return value
+
+
+def gather_level(block, axis, stride, count):
+    axis_size = lax.axis_size(axis)
+    mine = (lax.axis_index(axis) // stride) % count
+    whole = jnp.zeros((count,) + block.shape, block.dtype)
+    whole = lax.dynamic_update_index_in_dim(whole, block, mine, 0)
+    for shift in range(1, count):
+        piece = lax.ppermute(block, axis, pair_moves(axis_size, stride, count, shift))
+        whole = lax.dynamic_update_index_in_dim(whole, piece, (mine - shift) % count, 0)
+    return whole
+
+
+def gather_rows(block):
+    high, low = dp_levels()
+    whole = gather_level(block, "shard", 1, lax.axis_size("shard"))
+    whole = gather_level(whole, "dp", low, high)
+    whole = gather_level(whole, "dp", 1, low)
+    whole = jnp.moveaxis(whole, (0, 1, 2), (2, 1, 0))
+    return whole.reshape(-1, block.shape[1])
+
+
+def pack_mixer(projection, collector, router, scales, layer):
+    pieces = (collector[layer], router[layer], scales[layer])
+    spare = -sum(piece.shape[1] for piece in pieces) % 128
+    zeros = jnp.zeros((pieces[0].shape[0], spare), jnp.bfloat16)
+    return projection[layer], jnp.concatenate(pieces + (zeros,), axis=1)
+
+
+def cut_mixer(proj_full, packed, experts):
+    width = proj_full.shape[0]
+    return (
+        proj_full,
+        packed[:, :width],
+        packed[:, width : width + experts],
+        packed[:, width + experts : width + experts + 2],
+    )
+
+
+def fetch_first(projection, collector, router, scales):
+    proj, packed = pack_mixer(projection, collector, router, scales, 0)
+    thirds = jnp.split(proj, 3, axis=1)
+    packed_full = gather_rows(packed)
+    proj_full = jnp.concatenate([gather_rows(third) for third in thirds], axis=1)
+    return cut_mixer(proj_full, packed_full, router.shape[2])
+
+
+def fetch_later(projection, collector, router, scales, layer, after):
+    proj, packed = pack_mixer(projection, collector, router, scales, layer)
+    both = jnp.concatenate([proj, packed], axis=1)
+    both, after = lax.optimization_barrier((both, after))
+    whole = lax.all_gather(both, ("shard", "dp"), axis=0, tiled=True)
+    return cut_mixer(whole[:, : proj.shape[1]], whole[:, proj.shape[1] :], router.shape[2]), after
 
 
 def score_heads(queries, key_heads, bias_heads, same_segment):
@@ -199,9 +252,7 @@
     route_float = route_hot.astype(jnp.float32)
     residual = tokens.astype(jnp.float32)
     stored = []
-    gathered = [
-        fetch_mixer(projection, collector, router, scales, layer) for layer in range(layers)
-    ]
+    gathered = {0: fetch_first(projection, collector, router, scales)}
     for layer in range(layers):
         fetched = gathered[layer]
         proj_full, collect_full, router_full, scales_full = fetched
@@ -212,6 +263,10 @@
         packed = jnp.dot(hidden_one, proj_full, preferred_element_type=jnp.float32).astype(
             jnp.bfloat16
         )
+        if layer + 1 < layers:
+            gathered[layer + 1], packed = fetch_later(
+                projection, collector, router, scales, layer + 1, packed
+            )
         queries = packed[:, :model_width].reshape(tokens_dev, HEADS, HEAD_DIM)
         key_heads = packed[:, model_width : 2 * model_width].reshape(tokens_dev, HEADS, HEAD_DIM)
         value_heads = packed[:, 2 * model_width :].reshape(tokens_dev, HEADS, HEAD_DIM)
@@ -234,17 +289,11 @@
         gate_value = jnp.sum(gate_probs * route_float, axis=1) * retained
         sent = normed_two.astype(jnp.bfloat16)
         buffer = jnp.dot(slot_back, sent, preferred_element_type=jnp.float32).astype(jnp.bfloat16)
-        arrived = send_rows(buffer.reshape(experts, capacity, model_width)).reshape(
-            experts * capacity, model_width
-        )
-        rows_all = spread_rows(arrived)
+        rows_all = send_rows(buffer.reshape(experts, capacity, model_width))
         hidden_pre = jnp.dot(rows_all, upward[layer, 0], preferred_element_type=jnp.float32)
         hidden_act = jax.nn.gelu(hidden_pre).astype(jnp.bfloat16)
         partial_value = jnp.dot(hidden_act, downward[layer, 0], preferred_element_type=jnp.float32)
-        expert_sum = (
-            sum_hidden(partial_value).astype(jnp.bfloat16).reshape(experts, capacity, model_width)
-        )
-        returned = return_rows(expert_sum).reshape(experts * capacity, model_width)
+        returned = return_rows(partial_value)
         expert_tokens = jnp.dot(slot_hot, returned, preferred_element_type=jnp.float32)
         residual = middle + gate_value[:, None] * expert_tokens
         stored.append(
@@ -270,15 +319,9 @@
             )
         )
     grad_residual = cotangent.astype(jnp.float32)
-    offset_total = jnp.zeros((HEADS, 2 * tokens_dev - 1), jnp.float32)
-    proj_grads, collect_grads, router_grads, scale_grads, up_grads, down_grads = (
-        [],
-        [],
-        [],
-        [],
-        [],
-        [],
-    )
+    pair_total = jnp.zeros((HEADS, tokens_dev, tokens_dev), jnp.float32)
+    proj_grads, collect_grads, up_grads, down_grads = [], [], [], []
+    small_rows = []
     for layer in reversed(range(layers)):
         saved_layer = stored[layer]
         proj_full, collect_full, router_full, scales_full = saved_layer["fetched"]
@@ -292,10 +335,7 @@
         grad_buffer = jnp.dot(
             slot_back, grad_tokens_out, preferred_element_type=jnp.float32
         ).astype(jnp.bfloat16)
-        grad_arrived = send_rows(grad_buffer.reshape(experts, capacity, model_width)).reshape(
-            experts * capacity, model_width
-        )
-        grad_spread = spread_rows(grad_arrived)
+        grad_spread = send_rows(grad_buffer.reshape(experts, capacity, model_width))
         grad_act = jnp.dot(grad_spread, downward[layer, 0].T, preferred_element_type=jnp.float32)
         gelu_value, gelu_pull = jax.vjp(jax.nn.gelu, saved_layer["hidden_pre"])
         grad_pre = gelu_pull(grad_act)[0].astype(jnp.bfloat16)
@@ -304,16 +344,13 @@
         )
         grad_up = jnp.dot(saved_layer["rows_all"].T, grad_pre, preferred_element_type=jnp.float32)
         grad_sent_part = jnp.dot(grad_pre, upward[layer, 0].T, preferred_element_type=jnp.float32)
-        grad_sent = (
-            sum_hidden(grad_sent_part).astype(jnp.bfloat16).reshape(experts, capacity, model_width)
-        )
-        grad_back = return_rows(grad_sent).reshape(experts * capacity, model_width)
+        grad_back = return_rows(grad_sent_part)
         grad_normed_two = jnp.dot(slot_hot, grad_back, preferred_element_type=jnp.float32)
         grad_gprobs = (grad_gate * retained)[:, None] * route_float
         grad_logits = gate_probs * (
             grad_gprobs - jnp.sum(grad_gprobs * gate_probs, axis=1, keepdims=True)
         )
-        grad_router = jnp.dot(saved_layer["normed_two"].T, grad_logits, precision=HIGHEST)
+        grad_router_t = jnp.dot(grad_logits.T, saved_layer["normed_two"], precision=HIGHEST)
         grad_normed_two = grad_normed_two + jnp.dot(grad_logits, router_float.T, precision=HIGHEST)
         grad_mid_norm, grad_gain_two = rms_backward(
             grad_normed_two, gain_two, saved_layer["base_two"], saved_layer["scale_two"]
@@ -355,9 +392,7 @@
             jnp.einsum("hts,thd->shd", grad_scores_low, queries, preferred_element_type=jnp.float32)
             * head_scale
         )
-        offset_total = offset_total + pairs_to_offsets(
-            grad_scores_low.astype(jnp.float32), tokens_dev
-        )
+        pair_total = pair_total + grad_scores_low.astype(jnp.float32)
         grad_packed = jnp.concatenate(
             [
                 grad_queries.reshape(tokens_dev, model_width),
@@ -374,24 +409,30 @@
             grad_hidden_one, gain_one, saved_layer["base_one"], saved_layer["scale_one"]
         )
         grad_residual = grad_middle + grad_in_norm
-        grad_scales = jnp.stack([grad_gain_one, grad_gain_two], axis=1)
         expert_shares = reduce_experts(grad_up, grad_down_t)
-        shares = reduce_mixer([grad_proj, grad_collect, grad_router, grad_scales])
+        shares = (reduce_rows(grad_proj), reduce_rows(grad_collect))
+        small_rows = [grad_router_t, grad_gain_one[None], grad_gain_two[None]] + small_rows
         proj_grads.insert(0, shares[0])
         collect_grads.insert(0, shares[1])
-        router_grads.insert(0, shares[2])
-        scale_grads.insert(0, shares[3])
         up_grads.insert(0, expert_shares[0][None])
         down_grads.insert(0, expert_shares[1].T[None])
-    table_total = jnp.dot(offset_total, offset_hot, precision=HIGHEST).T
-    table_sum = lax.psum(table_total, ("expert", "shard", "dp"))
+    offset_total = pairs_to_offsets(pair_total, tokens_dev)
+    table_total = jnp.dot(offset_total, offset_hot, precision=HIGHEST)
+    table_rows = jnp.pad(table_total, ((0, 0), (0, model_width - buckets_all)))
+    small_sum = sum_everywhere(jnp.concatenate(small_rows + [table_rows]))
+    split = layers * (experts + 2)
+    table_sum = small_sum[split:, :buckets_all].T
+    width = router.shape[1]
+    owner = lax.axis_index("shard") * lax.axis_size("dp") + lax.axis_index("dp")
+    small_mine = lax.dynamic_slice_in_dim(small_sum[:split], owner * width, width, 1)
+    small_mine = jnp.swapaxes(small_mine.reshape(layers, experts + 2, width), 1, 2)
     return (
         residual.astype(jnp.bfloat16),
         grad_residual,
         jnp.stack(proj_grads),
         jnp.stack(collect_grads),
-        jnp.stack(router_grads),
-        jnp.stack(scale_grads),
+        small_mine[:, :, :experts],
+        small_mine[:, :, experts:],
         jnp.stack(up_grads),
         jnp.stack(down_grads),
         table_sum,

time: 652 us -> 560 us (0.86)
  blocking collectives: 189 us -> 0 us
  starting transfers between devices: 35.5 us -> 137 us
  waiting for transfers between devices: 216 us -> 250 us
  matrix products: 78.1 us -> 63 us
  local copies, waits for them, and re-layouts: 71.1 us -> 56.7 us
  other arithmetic: 36 us -> 27 us
    ppermute x2 -> x85, waiting for transfers between devices: 4.28 us -> 183 us  [the longest x24 69 us: return_rows(): lax.ppermute(parts[away, shift], 'shard', pair_moves(owners, 1, owners, o...]
    ppermute x2 -> x85, starting transfers between devices: 2.19 us -> 108 us  [the longest x24 36 us: return_rows(): lax.ppermute(parts[away, shift], 'shard', pair_moves(owners, 1, owners, o...]
    all_gather x2 -> x1, waiting for transfers between devices: 101 us -> 0.02 us  [fetch_later(): whole = lax.all_gather(both, ('shard', 'dp'), axis=0, tiled=True)]
    psum x1 -> x0, blocking collectives: 85.4 us -> none  [body(): table_sum = lax.psum(table_total, ('expert', 'shard', 'dp'))]
    all_gather x4 -> x0, blocking collectives: 79.7 us -> none  [spread_rows(): return lax.all_gather(arrived, 'shard', axis=0, tiled=True)]
    reduce_scatter x4 -> x0, waiting for transfers between devices: 62.2 us -> none  [sum_hidden(): lax.psum_scatter(partial_value.astype(jnp.bfloat16), 'shard', scatter_dim...]
    ppermute x16 -> x28, waiting for transfers between devices: 39.6 us -> 66.9 us  [scatter_sum(): lax.ppermute(leaving, axis, pair_moves(axis_size, stride, count, shift))]
    all_to_all x3 -> x0, blocking collectives: 23.6 us -> none  [send_rows(): lax.all_to_all(buffer, 'expert', split_axis=0, concat_axis=0, tiled=True)]
  transfers between devices with their start and end apart: 29 -> 114, of which waited for: 16 -> 63; matrix products, arithmetic and copies ran while one was open for 12% -> 16% of each run, Pallas kernels for 0% -> 0%
where the time goes in v2:
time: 560 us; the launch traced here: 550 us
  waiting for transfers between devices  250 us (45%)
  starting transfers between devices  137 us (24%)
  matrix products  63 us (11%)
  local copies, waits for them, and re-layouts  56.7 us (10%)
  other arithmetic  27 us (5%)
  between operations  17 us (3%)
    ppermute x24, waiting for transfers between devices, return_rows(): lax.ppermute(parts[away, shift], 'shard', pair_moves(owners, 1, owners, o...  69 us
    ppermute x28, waiting for transfers between devices, scatter_sum(): lax.ppermute(leaving, axis, pair_moves(axis_size, stride, count, shift))  66.9 us
    ppermute x24, waiting for transfers between devices, send_rows(): lax.ppermute(piece, 'shard', pair_moves(owners, 1, owners, shift))  45.6 us
    ppermute x20, waiting for transfers between devices, gather_level(): lax.ppermute(block, axis, pair_moves(axis_size, stride, count, shift))  39.9 us
    ppermute x24, starting transfers between devices, return_rows(): lax.ppermute(parts[away, shift], 'shard', pair_moves(owners, 1, owners, o...  36 us
    ppermute x24, starting transfers between devices, send_rows(): lax.ppermute(piece, 'shard', pair_moves(owners, 1, owners, shift))  35 us
    ppermute x28, starting transfers between devices, scatter_sum(): lax.ppermute(leaving, axis, pair_moves(axis_size, stride, count, shift))  29.5 us
    ppermute x20, starting transfers between devices, gather_level(): lax.ppermute(block, axis, pair_moves(axis_size, stride, count, shift))  18.7 us
  transfers between devices with their start and end apart: 114, of which 63 were waited for; matrix products, arithmetic and copies ran while one was open for 16% of the time, Pallas kernels for 0%

profile of v2, /device:TPU:0, one launch (start us, length us, event | category | flops | bytes accessed | tf_op | source)
XLA Modules:
  0.0 550.4 jit_solution(3005733310284554406)
XLA Ops:
  29.2 4.2 collective-permute-start.11
  56.2 6.2 %collective-permute-done.13 = bf16[4,48,768]{2,1,0:T(8,128)(2,1)S(1)} collective-permute-done((bf16[4,48,768]{2,1,0:T(8,128)(2,1)S(1)}, bf16[4,48,768]{2,1,0:T(8,128)(2,1)S(1)}, u32[]{:S(2)}, u32[]{:S(2)}) %collective-permute-start.13) | collective-permute-done | bytes 294944 | tf_op jit(solution)/shard_map/ppermute | solution.py:140
  62.8 4.5 collective-permute-done.18
  109.9 17.4 %collective-permute-done.25 = bf16[80,768]{1,0:T(8,128)(2,1)S(1)} collective-permute-done((bf16[80,768]{1,0:T(8,128)(2,1)S(1)}, bf16[80,768]{1,0:T(8,128)(2,1)S(1)}, u32[]{:S(2)}, u32[]{:S(2)}) %collective-permute-start.25) | collective-permute-done | bytes 122912 | tf_op jit(solution)/shard_map/ppermute | solution.py:48
  131.3 7.6 %collective-permute-start.27 = (bf16[80,768]{1,0:T(8,128)(2,1)S(1)}, bf16[80,768]{1,0:T(8,128)(2,1)S(1)}, u32[]{:S(2)}, u32[]{:S(2)}) collective-permute-start(bf16[80,768]{1,0:T(8,128)(2,1)S(1)} %get-tuple-element.85), channel_id=1, source_target_pairs={{0,12},{4,0},{8,4},{12,8},{1,13},{5,1},{9,5},{13,9},{2,14},{6,2},{... | collective-permute-start | bytes 368648 | tf_op jit(solution)/shard_map/ppermute | solution.py:61
  142.6 8.5 %collective-permute-done.28 = bf16[80,768]{1,0:T(8,128)(2,1)S(1)} collective-permute-done((bf16[80,768]{1,0:T(8,128)(2,1)S(1)}, bf16[80,768]{1,0:T(8,128)(2,1)S(1)}, u32[]{:S(2)}, u32[]{:S(2)}) %collective-permute-start.28) | collective-permute-done | bytes 122912 | tf_op jit(solution)/shard_map/ppermute | solution.py:61
  158.4 5.4 collective-permute-done.32
  191.9 5.0 collective-permute-done.35
  198.4 5.8 %collective-permute-done.39 = bf16[80,768]{1,0:T(8,128)(2,1)S(1)} collective-permute-done((bf16[80,768]{1,0:T(8,128)(2,1)S(1)}, bf16[80,768]{1,0:T(8,128)(2,1)S(1)}, u32[]{:S(2)}, u32[]{:S(2)}) %collective-permute-start.39) | collective-permute-done | bytes 122912 | tf_op jit(solution)/shard_map/ppermute | solution.py:48
  210.1 4.2 collective-permute-start.41
  218.4 6.6 %collective-permute-done.42 = bf16[80,768]{1,0:T(8,128)(2,1)} collective-permute-done((bf16[80,768]{1,0:T(8,128)(2,1)}, bf16[80,768]{1,0:T(8,128)(2,1)}, u32[]{:S(2)}, u32[]{:S(2)}) %collective-permute-start.42) | collective-permute-done | bytes 122912 | tf_op jit(solution)/shard_map/ppermute | solution.py:61
  235.0 6.6 %collective-permute-done.46 = bf16[80,768]{1,0:T(8,128)(2,1)S(1)} collective-permute-done((bf16[80,768]{1,0:T(8,128)(2,1)}, bf16[80,768]{1,0:T(8,128)(2,1)S(1)}, u32[]{:S(2)}, u32[]{:S(2)}) %collective-permute-start.46) | collective-permute-done | bytes 122912 | tf_op jit(solution)/shard_map/ppermute | solution.py:61
  266.7 5.3 collective-permute-start.55
  275.7 5.6 %collective-permute-done.56 = bf16[80,768]{1,0:T(8,128)(2,1)S(1)} collective-permute-done((bf16[80,768]{1,0:T(8,128)(2,1)S(1)}, bf16[80,768]{1,0:T(8,128)(2,1)S(1)}, u32[]{:S(2)}, u32[]{:S(2)}) %collective-permute-start.56) | collective-permute-done | bytes 122912 | tf_op jit(solution)/shard_map/ppermute | solution.py:61
  289.5 7.0 %collective-permute-done.60 = bf16[80,768]{1,0:T(8,128)(2,1)S(1)} collective-permute-done((bf16[80,768]{1,0:T(8,128)(2,1)S(1)}, bf16[80,768]{1,0:T(8,128)(2,1)S(1)}, u32[]{:S(2)}, u32[]{:S(2)}) %collective-permute-start.60) | collective-permute-done | bytes 122912 | tf_op jit(solution)/shard_map/ppermute | solution.py:61
  347.9 7.3 %collective-permute-done.70 = bf16[80,768]{1,0:T(8,128)(2,1)S(1)} collective-permute-done((bf16[80,768]{1,0:T(8,128)(2,1)S(1)}, bf16[80,768]{1,0:T(8,128)(2,1)S(1)}, u32[]{:S(2)}, u32[]{:S(2)}) %collective-permute-start.70) | collective-permute-done | bytes 122912 | tf_op jit(solution)/shard_map/ppermute | solution.py:61
  367.1 5.7 %collective-permute-done.74 = bf16[80,768]{1,0:T(8,128)(2,1)S(1)} collective-permute-done((bf16[80,768]{1,0:T(8,128)(2,1)S(1)}, bf16[80,768]{1,0:T(8,128)(2,1)S(1)}, u32[]{:S(2)}, u32[]{:S(2)}) %collective-permute-start.74) | collective-permute-done | bytes 122912 | tf_op jit(solution)/shard_map/ppermute | solution.py:61
  424.2 7.8 %collective-permute-done.91 = bf16[4,2,48,384]{3,2,0,1:T(8,128)(2,1)S(1)} collective-permute-done((bf16[4,2,48,384]{3,2,0,1:T(8,128)(2,1)S(1)}, bf16[4,2,48,384]{3,2,0,1:T(8,128)(2,1)S(1)}, u32[]{:S(2)}, u32[]{:S(2)}) %collective-permute-start.91) | collective-permute-done | bytes 294944 | tf_op jit(solution)/shard_map/ppermute | solution.py:77
  432.9 7.2 %collective-permute-done.98 = bf16[4,2,48,384]{3,2,0,1:T(8,128)(2,1)S(1)} collective-permute-done((bf16[4,2,48,384]{3,2,0,1:T(8,128)(2,1)S(1)}, bf16[4,2,48,384]{3,2,0,1:T(8,128)(2,1)S(1)}, u32[]{:S(2)}, u32[]{:S(2)}) %collective-permute-start.98) | collective-permute-done | bytes 294944 | tf_op jit(solution)/shard_map/ppermute | solution.py:77
  468.1 5.6 %collective-permute-done.110 = bf16[2,192,768]{2,1,0:T(8,128)(2,1)S(1)} collective-permute-done((bf16[2,192,768]{2,1,0:T(8,128)(2,1)S(1)}, bf16[2,192,768]{2,1,0:T(8,128)(2,1)S(1)}, u32[]{:S(2)}, u32[]{:S(2)}) %collective-permute-start.110) | collective-permute-done | bytes 589856 | tf_op jit(solution)/shard_map/ppermute | solution.py:77
  473.9 7.3 %collective-permute-done.112 = bf16[2,192,768]{2,1,0:T(8,128)(2,1)S(1)} collective-permute-done((bf16[2,192,768]{2,1,0:T(8,128)(2,1)S(1)}, bf16[2,192,768]{2,1,0:T(8,128)(2,1)S(1)}, u32[]{:S(2)}, u32[]{:S(2)}) %collective-permute-start.112) | collective-permute-done | bytes 589856 | tf_op jit(solution)/shard_map/ppermute | solution.py:77
  487.6 18.4 %collective-permute-done.77 = bf16[4,2,48,1152]{3,2,0,1:T(8,128)(2,1)S(1)} collective-permute-done((bf16[4,2,48,1152]{3,2,0,1:T(8,128)(2,1)S(1)}, bf16[4,2,48,1152]{3,2,0,1:T(8,128)(2,1)S(1)}, u32[]{:S(2)}, u32[]{:S(2)}) %collective-permute-start.77) | collective-permute-done | bytes 884768 | tf_op jit(solution)/shard_map/ppermute | solution.py:77
  507.3 11.6 %collective-permute-done.84 = bf16[4,2,48,1152]{3,2,0,1:T(8,128)(2,1)S(1)} collective-permute-done((bf16[4,2,48,1152]{3,2,0,1:T(8,128)(2,1)S(1)}, bf16[4,2,48,1152]{3,2,0,1:T(8,128)(2,1)S(1)}, u32[]{:S(2)}, u32[]{:S(2)}) %collective-permute-start.84) | collective-permute-done | bytes 884768 | tf_op jit(solution)/shard_map/ppermute | solution.py:77
  538.4 4.0 collective-permute-done.89
  (700 shorter events, 358.8 us)
Async XLA Ops:
  7.2 157.7 %all-gather.2.cloned.1.call-start = ((), (), s32[]{:S(2)}) async-start(), calls=%async_computation | async-start | bytes 5222400 | tf_op jit(solution)/shard_map/all_gather | solution.py:183
  9.9 39.9 %collective-permute-start = (bf16[48,896]{1,0:T(8,128)(2,1)S(1)}, bf16[48,896]{1,0:T(8,128)(2,1)S(1)}, u32[]{:S(2)}, u32[]{:S(2)}) collective-permute-start(bf16[48,896]{1,0:T(8,128)(2,1)S(1)} %get-tuple-element.45), channel_id=1, source_target_pairs={{0,4},{4,8},{8,12},{12,0},{1,5},{5,9},{9,13},{13,1},{2,6},{6,10},{... | collective-permute-start | bytes 258056 | tf_op jit(solution)/shard_map/ppermute | solution.py:140
  13.0 37.6 %collective-permute-start.1 = (bf16[48,896]{1,0:T(8,128)(2,1)S(1)}, bf16[48,896]{1,0:T(8,128)(2,1)S(1)}, u32[]{:S(2)}, u32[]{:S(2)}) collective-permute-start(bf16[48,896]{1,0:T(8,128)(2,1)S(1)} %get-tuple-element.45), channel_id=1, source_target_pairs={{0,8},{4,12},{8,0},{12,4},{1,9},{5,13},{9,1},{13,5},{2,10},{6,14},... | collective-permute-start | bytes 258056 | tf_op jit(solution)/shard_map/ppermute | solution.py:140
  15.6 35.1 %collective-permute-start.2 = (bf16[48,896]{1,0:T(8,128)(2,1)S(1)}, bf16[48,896]{1,0:T(8,128)(2,1)S(1)}, u32[]{:S(2)}, u32[]{:S(2)}) collective-permute-start(bf16[48,896]{1,0:T(8,128)(2,1)S(1)} %get-tuple-element.45), channel_id=1, source_target_pairs={{0,12},{4,0},{8,4},{12,8},{1,13},{5,1},{9,5},{13,9},{2,14},{6,2},{... | collective-permute-start | bytes 258056 | tf_op jit(solution)/shard_map/ppermute | solution.py:140
  49.8 17.5 %collective-permute-start.18 = (bf16[4,48,768]{2,1,0:T(8,128)(2,1)S(1)}, bf16[4,48,768]{2,1,0:T(8,128)(2,1)S(1)}, u32[]{:S(2)}, u32[]{:S(2)}) collective-permute-start(bf16[4,48,768]{2,1,0:T(8,128)(2,1)S(1)} %bitcast_dynamic-update-slice_fusion.24), channel_id=1, source_target_pairs={{0,2},{1,3},{2,0},{3,1},{4,6},{5,7},{6,4},{7,5},{8,10},{9,11},{10,... | collective-permute-start | bytes 884744 | tf_op jit(solution)/shard_map/ppermute | solution.py:140
  50.7 20.3 %collective-permute-start.3 = (bf16[4,48,896]{2,1,0:T(8,128)(2,1)S(1)}, bf16[4,48,896]{2,1,0:T(8,128)(2,1)S(1)}, u32[]{:S(2)}, u32[]{:S(2)}) collective-permute-start(bf16[4,48,896]{2,1,0:T(8,128)(2,1)S(1)} %bitcast_dynamic-update-slice_fusion.20), channel_id=1, source_target_pairs={{0,2},{1,3},{2,0},{3,1},{4,6},{5,7},{6,4},{7,5},{8,10},{9,11},{10,... | collective-permute-start | bytes 1032200 | tf_op jit(solution)/shard_map/ppermute | solution.py:140
  56.1 15.2 %collective-permute-start.9 = (bf16[2,4,48,768]{3,2,0,1:T(8,128)(2,1)S(1)}, bf16[2,4,48,768]{3,2,0,1:T(8,128)(2,1)S(1)}, u32[]{:S(2)}, u32[]{:S(2)}) collective-permute-start(bf16[2,4,48,768]{3,2,0,1:T(8,128)(2,1)S(1)} %bitcast_dynamic-update-slice_fusion.15), channel_id=1, source_target_pairs={{0,1},{1,0},{2,3},{3,2},{4,5},{5,4},{6,7},{7,6},{8,9},{9,8},{10,11... | collective-permute-start | bytes 1769480 | tf_op jit(solution)/shard_map/ppermute | solution.py:140
  103.7 23.6 %collective-permute-start.25 = (bf16[80,768]{1,0:T(8,128)(2,1)S(1)}, bf16[80,768]{1,0:T(8,128)(2,1)S(1)}, u32[]{:S(2)}, u32[]{:S(2)}) collective-permute-start(bf16[80,768]{1,0:T(8,128)(2,1)S(1)} %collective-permute-done.23), channel_id=1, source_target_pairs={{0,8},{4,12},{8,0},{12,4},{1,9},{5,13},{9,1},{13,5},{2,10},{6,14},... | collective-permute-start | bytes 368648 | tf_op jit(solution)/shard_map/ppermute | solution.py:48
  103.7 23.5 %collective-permute-start.26 = (bf16[80,768]{1,0:T(8,128)(2,1)S(1)}, bf16[80,768]{1,0:T(8,128)(2,1)S(1)}, u32[]{:S(2)}, u32[]{:S(2)}) collective-permute-start(bf16[80,768]{1,0:T(8,128)(2,1)S(1)} %collective-permute-done.23), channel_id=1, source_target_pairs={{0,12},{4,0},{8,4},{12,8},{1,13},{5,1},{9,5},{13,9},{2,14},{6,2},{... | collective-permute-start | bytes 368648 | tf_op jit(solution)/shard_map/ppermute | solution.py:48
  182.5 14.4 %collective-permute-start.35 = (bf16[80,768]{1,0:T(8,128)(2,1)S(1)}, bf16[80,768]{1,0:T(8,128)(2,1)S(1)}, u32[]{:S(2)}, u32[]{:S(2)}) collective-permute-start(bf16[80,768]{1,0:T(8,128)(2,1)S(1)} %get-tuple-element.37), channel_id=1, source_target_pairs={{0,8},{4,12},{8,0},{12,4},{1,9},{5,13},{9,1},{13,5},{2,10},{6,14},... | collective-permute-start | bytes 368648 | tf_op jit(solution)/shard_map/ppermute | solution.py:48
  187.0 17.2 %collective-permute-start.39 = (bf16[80,768]{1,0:T(8,128)(2,1)S(1)}, bf16[80,768]{1,0:T(8,128)(2,1)S(1)}, u32[]{:S(2)}, u32[]{:S(2)}) collective-permute-start(bf16[80,768]{1,0:T(8,128)(2,1)S(1)} %collective-permute-done.37), channel_id=1, source_target_pairs={{0,8},{4,12},{8,0},{12,4},{1,9},{5,13},{9,1},{13,5},{2,10},{6,14},... | collective-permute-start | bytes 368648 | tf_op jit(solution)/shard_map/ppermute | solution.py:48
  312.7 15.4 %collective-permute-start.62 = (bf16[80,768]{1,0:T(8,128)(2,1)S(1)}, bf16[80,768]{1,0:T(8,128)(2,1)S(1)}, u32[]{:S(2)}, u32[]{:S(2)}) collective-permute-start(bf16[80,768]{1,0:T(8,128)(2,1)S(1)} %get-tuple-element.30), channel_id=1, source_target_pairs={{0,4},{4,8},{8,12},{12,0},{1,5},{5,9},{9,13},{13,1},{2,6},{6,10},{... | collective-permute-start | bytes 368648 | tf_op jit(solution)/shard_map/ppermute | solution.py:48
  312.8 18.2 %collective-permute-start.63 = (bf16[80,768]{1,0:T(8,128)(2,1)S(1)}, bf16[80,768]{1,0:T(8,128)(2,1)S(1)}, u32[]{:S(2)}, u32[]{:S(2)}) collective-permute-start(bf16[80,768]{1,0:T(8,128)(2,1)S(1)} %get-tuple-element.30), channel_id=1, source_target_pairs={{0,8},{4,12},{8,0},{12,4},{1,9},{5,13},{9,1},{13,5},{2,10},{6,14},... | collective-permute-start | bytes 368648 | tf_op jit(solution)/shard_map/ppermute | solution.py:48
  314.2 16.8 %collective-permute-start.64 = (bf16[80,768]{1,0:T(8,128)(2,1)S(1)}, bf16[80,768]{1,0:T(8,128)(2,1)S(1)}, u32[]{:S(2)}, u32[]{:S(2)}) collective-permute-start(bf16[80,768]{1,0:T(8,128)(2,1)S(1)} %get-tuple-element.30), channel_id=1, source_target_pairs={{0,12},{4,0},{8,4},{12,8},{1,13},{5,1},{9,5},{13,9},{2,14},{6,2},{... | collective-permute-start | bytes 368648 | tf_op jit(solution)/shard_map/ppermute | solution.py:48
  359.4 81.6 %collective-permute-start.109 = (bf16[2,2,192,768]{3,2,0,1:T(8,128)(2,1)}, bf16[2,2,192,768]{3,2,0,1:T(8,128)(2,1)}, u32[]{:S(2)}, u32[]{:S(2)}) collective-permute-start(bf16[2,2,192,768]{3,2,0,1:T(8,128)(2,1)} %bitcast.574), channel_id=1, source_target_pairs={{0,1},{1,0},{2,3},{3,2},{4,5},{5,4},{6,7},{7,6},{8,9},{9,8},{10,11... | collective-permute-start | bytes 3538952 | tf_op jit(solution)/shard_map/ppermute | solution.py:77
  360.5 83.5 %collective-permute-start.111 = (bf16[2,2,192,768]{3,2,0,1:T(8,128)(2,1)}, bf16[2,2,192,768]{3,2,0,1:T(8,128)(2,1)}, u32[]{:S(2)}, u32[]{:S(2)}) collective-permute-start(bf16[2,2,192,768]{3,2,0,1:T(8,128)(2,1)} %bitcast.573), channel_id=1, source_target_pairs={{0,1},{1,0},{2,3},{3,2},{4,5},{5,4},{6,7},{7,6},{8,9},{9,8},{10,11... | collective-permute-start | bytes 3538952 | tf_op jit(solution)/shard_map/ppermute | solution.py:77
  402.2 20.0 %collective-permute-start.90 = (bf16[4,2,48,768]{3,2,0,1:T(8,128)(2,1)S(1)}, bf16[4,2,48,768]{3,2,0,1:T(8,128)(2,1)S(1)}, u32[]{:S(2)}, u32[]{:S(2)}) collective-permute-start(bf16[4,2,48,768]{3,2,0,1:T(8,128)(2,1)S(1)} %bitcast.657), channel_id=1, source_target_pairs={{0,1},{1,0},{2,3},{3,2},{4,5},{5,4},{6,7},{7,6},{8,9},{9,8},{10,11... | collective-permute-start | bytes 1769480 | tf_op jit(solution)/shard_map/ppermute | solution.py:77
  402.4 20.6 %collective-permute-start.97 = (bf16[4,2,48,768]{3,2,0,1:T(8,128)(2,1)S(1)}, bf16[4,2,48,768]{3,2,0,1:T(8,128)(2,1)S(1)}, u32[]{:S(2)}, u32[]{:S(2)}) collective-permute-start(bf16[4,2,48,768]{3,2,0,1:T(8,128)(2,1)S(1)} %bitcast.656), channel_id=1, source_target_pairs={{0,1},{1,0},{2,3},{3,2},{4,5},{5,4},{6,7},{7,6},{8,9},{9,8},{10,11... | collective-permute-start | bytes 1769480 | tf_op jit(solution)/shard_map/ppermute | solution.py:77
  420.9 61.5 %collective-permute-start.76 = (bf16[4,2,48,2304]{3,2,0,1:T(8,128)(2,1)S(1)}, bf16[4,2,48,2304]{3,2,0,1:T(8,128)(2,1)S(1)}, u32[]{:S(2)}, u32[]{:S(2)}) collective-permute-start(bf16[4,2,48,2304]{3,2,0,1:T(8,128)(2,1)S(1)} %bitcast.595), channel_id=1, source_target_pairs={{0,1},{1,0},{2,3},{3,2},{4,5},{5,4},{6,7},{7,6},{8,9},{9,8},{10,11... | collective-permute-start | bytes 5308424 | tf_op jit(solution)/shard_map/ppermute | solution.py:77
  422.2 62.0 %collective-permute-start.83 = (bf16[4,2,48,2304]{3,2,0,1:T(8,128)(2,1)S(1)}, bf16[4,2,48,2304]{3,2,0,1:T(8,128)(2,1)S(1)}, u32[]{:S(2)}, u32[]{:S(2)}) collective-permute-start(bf16[4,2,48,2304]{3,2,0,1:T(8,128)(2,1)S(1)} %bitcast.594), channel_id=1, source_target_pairs={{0,1},{1,0},{2,3},{3,2},{4,5},{5,4},{6,7},{7,6},{8,9},{9,8},{10,11... | collective-permute-start | bytes 5308424 | tf_op jit(solution)/shard_map/ppermute | solution.py:77
  457.4 16.3 %collective-permute-start.110 = (bf16[2,192,768]{2,1,0:T(8,128)(2,1)S(1)}, bf16[2,192,768]{2,1,0:T(8,128)(2,1)S(1)}, u32[]{:S(2)}, u32[]{:S(2)}) collective-permute-start(bf16[2,192,768]{2,1,0:T(8,128)(2,1)S(1)} %dynamic-slice_bitcast_fusion.1), channel_id=1, source_target_pairs={{0,2},{1,3},{2,0},{3,1},{4,6},{5,7},{6,4},{7,5},{8,10},{9,11},{10,... | collective-permute-start | bytes 1769480 | tf_op jit(solution)/shard_map/ppermute | solution.py:77
  458.1 23.0 %collective-permute-start.112 = (bf16[2,192,768]{2,1,0:T(8,128)(2,1)S(1)}, bf16[2,192,768]{2,1,0:T(8,128)(2,1)S(1)}, u32[]{:S(2)}, u32[]{:S(2)}) collective-permute-start(bf16[2,192,768]{2,1,0:T(8,128)(2,1)S(1)} %dynamic-slice_bitcast_fusion), channel_id=1, source_target_pairs={{0,2},{1,3},{2,0},{3,1},{4,6},{5,7},{6,4},{7,5},{8,10},{9,11},{10,... | collective-permute-start | bytes 1769480 | tf_op jit(solution)/shard_map/ppermute | solution.py:77
  483.4 22.6 %collective-permute-start.77 = (bf16[4,2,48,1152]{3,2,0,1:T(8,128)(2,1)S(1)}, bf16[4,2,48,1152]{3,2,0,1:T(8,128)(2,1)S(1)}, u32[]{:S(2)}, u32[]{:S(2)}) collective-permute-start(bf16[4,2,48,1152]{3,2,0,1:T(8,128)(2,1)S(1)} %fusion.73), channel_id=1, source_target_pairs={{0,16},{16,0},{1,17},{17,1},{2,18},{18,2},{3,19},{19,3},{4,20},{20... | collective-permute-start | bytes 2654216 | tf_op jit(solution)/shard_map/ppermute | solution.py:77
  485.2 33.7 %collective-permute-start.84 = (bf16[4,2,48,1152]{3,2,0,1:T(8,128)(2,1)S(1)}, bf16[4,2,48,1152]{3,2,0,1:T(8,128)(2,1)S(1)}, u32[]{:S(2)}, u32[]{:S(2)}) collective-permute-start(bf16[4,2,48,1152]{3,2,0,1:T(8,128)(2,1)S(1)} %fusion.69), channel_id=1, source_target_pairs={{0,16},{16,0},{1,17},{17,1},{2,18},{18,2},{3,19},{19,3},{4,20},{20... | collective-permute-start | bytes 2654216 | tf_op jit(solution)/shard_map/ppermute | solution.py:77
  (188 other events, 1580.6 us)
Sparse Core Ops, SparseCore 0:
  75.4 64.2 all-gather.1
